TPU v7x, 256 devices: a whole 4x4x8 slice. The times are simulated.
256 devices in a mesh: seq: 32 (over y, z), dp: 8 (over x, core).
Axes of the slice: x: 4, y: 4, z: 8, core: 2. Of those that a mesh axis runs over, the one named last changes fastest.
Arguments:
- queries: bfloat16 [16384, 8192], P('seq', 'dp'), may hold values from -6 to 6
- key_vecs: bfloat16 [16384, 8192], P('seq', 'dp'), may hold values from -0.5 to 0.5
- value_vecs: bfloat16 [16384, 8192], P('seq', 'dp'), may hold values from -6 to 6
- log_decay: float32 [16384, 64], P('seq', 'dp'), may hold values from -2 to 0, as said below
- norm_gain: float32 [8192], P('dp'), may hold values from 0.5 to 1.5
- out_grad: bfloat16 [16384, 8192], P('seq', 'dp'), may hold values from -6 to 6
Outputs:
- normed: bfloat16 [16384, 8192], P('seq', 'dp')
- query_grad: bfloat16 [16384, 8192], P('seq', 'dp')
- key_grad: bfloat16 [16384, 8192], P('seq', 'dp')
- value_grad: bfloat16 [16384, 8192], P('seq', 'dp')
- gain_grad: float32 [8192], P('dp')
Inputs may be any that keep to these rules, and one draw needn't show every extreme that they name: `log_decay`: never positive.
All inputs are finite; a program needn't handle non-finite values.
Results may differ from a plain program's by a relative error of at most 0.0051.
Values sent between devices are 32-bit elements; how exact they have to be, the bound alone decides.
No kernel may reach another device: no remote copies, remote signals or barrier semaphores. Data moves between devices by JAX's collectives and lax.ppermute only.
A program may use at most 128 MiB of HBM per device.

v0:
```python
import jax
import jax.numpy as jnp
from jax import lax
from jax.sharding import PartitionSpec as P

BLOCK = 512


EPSILON = 1e-06
HIGH = lax.Precision.HIGHEST


def carried_in(x, axis, combine, identity, reverse):
    count, here = (lax.axis_size(axis), lax.axis_index(axis))
    everything = jax.tree.map(lambda part: lax.all_gather(part, axis), x)
    start = jax.tree.map(
        lambda part, zero: jnp.broadcast_to(jnp.asarray(zero, part.dtype), part.shape), x, identity
    )

    def hop(k, before):
        at = count - 1 - k if reverse else k
        reached = at > here if reverse else at < here
        new = combine(before, jax.tree.map(lambda part: part[at], everything))
        return jax.tree.map(lambda a, b: jnp.where(reached, a, b), new, before)

    return lax.fori_loop(0, count, hop, start)


def decay_table(cumul):
    length = cumul.shape[1]
    place = jnp.arange(length, dtype=jnp.int32)
    lower = (place[:, None] >= place[None, :])[None, :, :]
    spread = cumul[:, :, None] - cumul[:, None, :]
    return jnp.where(lower, jnp.exp(jnp.where(lower, spread, jnp.float32(0.0))), jnp.float32(0.0))


def intra_forward(carry, item):
    q_blk, k_blk, v_blk, a_blk = item
    cumul = jnp.cumsum(a_blk, axis=0).T
    weights = decay_table(cumul)
    score_matrix = jnp.einsum("thd,shd->hts", q_blk, k_blk, preferred_element_type=jnp.float32)
    probs = (weights * score_matrix).astype(jnp.bfloat16)
    result = jnp.einsum("hts,shd->thd", probs, v_blk, preferred_element_type=jnp.float32)
    tail = jnp.exp(cumul[:, -1:] - cumul).T[:, :, None]
    update = jnp.einsum(
        "shd,she->hde", tail * k_blk.astype(jnp.float32), v_blk.astype(jnp.float32), precision=HIGH
    )
    return (carry, (result, probs, update))


def intra_backward(carry, item):
    q_blk, k_blk, v_blk, a_blk, g_blk, probs = item
    cumul = jnp.cumsum(a_blk, axis=0).T
    weights = decay_table(cumul)
    errs = (
        weights * jnp.einsum("thd,shd->hts", g_blk, v_blk, preferred_element_type=jnp.float32)
    ).astype(jnp.bfloat16)
    dquery = jnp.einsum("hts,shd->thd", errs, k_blk, preferred_element_type=jnp.float32)
    dkey = jnp.einsum("hts,thd->shd", errs, q_blk, preferred_element_type=jnp.float32)
    dvalue = jnp.einsum("hts,thd->shd", probs, g_blk, preferred_element_type=jnp.float32)
    scaled = jnp.exp(cumul).T[:, :, None] * q_blk.astype(jnp.float32)
    update = jnp.einsum("thi,thj->hij", scaled, g_blk.astype(jnp.float32), precision=HIGH)
    return (carry, (dquery, dkey, dvalue, update))


def chain_step(state, item):
    update, last_log = item
    return (jnp.exp(last_log)[:, None, None] * state + update, state)


def combine(earlier, later):
    return (earlier[0] * later[0], later[0][:, None, None] * earlier[1] + later[1])


def on_device(queries, key_vecs, value_vecs, log_decay, norm_gain, out_grad):
    tok_rows = queries.shape[0]
    heads_here = log_decay.shape[1]
    width = queries.shape[1] // heads_here
    blocks = tok_rows // BLOCK
    four = (blocks, BLOCK, heads_here, width)
    q_blocks = queries.reshape(four)
    k_blocks = key_vecs.reshape(four)
    v_blocks = value_vecs.reshape(four)
    a_blocks = log_decay.reshape(blocks, BLOCK, heads_here)
    blocked = (q_blocks, k_blocks, v_blocks, a_blocks)
    zero_state = jnp.zeros((heads_here, width, width), jnp.float32)
    dummy = jnp.float32(0.0)
    unused, (results, probs, updates) = lax.scan(intra_forward, dummy, blocked)
    cumul_blk = jnp.cumsum(a_blocks, axis=1)
    lasts = cumul_blk[:, -1, :]
    total = jnp.sum(lasts, axis=0)
    through = jnp.exp(total)
    local_state, unused_states = lax.scan(chain_step, zero_state, (updates, lasts))
    identity = (jnp.ones((heads_here,), jnp.float32), zero_state)
    incoming = carried_in((through, local_state), "seq", combine, identity, False)[1]
    unused_end, state_in = lax.scan(chain_step, incoming, (updates, lasts))
    grow = jnp.exp(cumul_blk)[:, :, :, None]
    propagated_summary = jnp.einsum(
        "bthd,bhde->bthe", q_blocks.astype(jnp.float32), state_in, precision=HIGH
    )
    attn = (results + grow * propagated_summary).reshape(tok_rows, heads_here * width)
    grad_flat = out_grad.astype(jnp.float32)
    squares = jnp.sum(attn * attn, axis=1)
    gdot_part = jnp.sum(norm_gain[None, :] * grad_flat * attn, axis=1)
    squares, gdot = lax.psum((squares, gdot_part), "dp")
    features = heads_here * width * lax.axis_size("dp")
    inv_rms = lax.rsqrt(squares / features + EPSILON)[:, None]
    normed = (attn * inv_rms * norm_gain[None, :]).astype(jnp.bfloat16)
    gain_part = jnp.sum(grad_flat * attn * inv_rms, axis=0)
    gain_grad = lax.psum(gain_part, "seq")
    attn_grad = (
        inv_rms * norm_gain[None, :] * grad_flat - attn * inv_rms**3 * gdot[:, None] / features
    ).astype(jnp.bfloat16)
    g_blocks = attn_grad.reshape(four)
    back_items = blocked + (g_blocks, probs)
    unused_back, (dquery, dkey, dvalue, state_flow_changes) = lax.scan(
        intra_backward, dummy, back_items
    )
    local_flow, unused_flows = lax.scan(
        chain_step, zero_state, (state_flow_changes, lasts), reverse=True
    )
    outflow = carried_in((through, local_flow), "seq", combine, identity, True)[1]
    unused_first, flow_in = lax.scan(chain_step, outflow, (state_flow_changes, lasts), reverse=True)
    tail = jnp.exp(lasts[:, None, :] - cumul_blk)[:, :, :, None]
    dquery = dquery + grow * jnp.einsum(
        "bthj,bhij->bthi", g_blocks.astype(jnp.float32), state_in, precision=HIGH
    )
    dkey = dkey + tail * jnp.einsum(
        "bthj,bhij->bthi", v_blocks.astype(jnp.float32), flow_in, precision=HIGH
    )
    dvalue = dvalue + tail * jnp.einsum(
        "bthi,bhij->bthj", k_blocks.astype(jnp.float32), flow_in, precision=HIGH
    )
    shape_out = (tok_rows, heads_here * width)
    return (
        normed,
        dquery.reshape(shape_out).astype(jnp.bfloat16),
        dkey.reshape(shape_out).astype(jnp.bfloat16),
        dvalue.reshape(shape_out).astype(jnp.bfloat16),
        gain_grad,
    )


def solution(mesh):
    placed = (
        P("seq", "dp"),
        P("seq", "dp"),
        P("seq", "dp"),
        P("seq", "dp"),
        P("dp"),
        P("seq", "dp"),
    )
    return jax.shard_map(
        on_device,
        mesh=mesh,
        in_specs=placed,
        out_specs=(P("seq", "dp"), P("seq", "dp"), P("seq", "dp"), P("seq", "dp"), P("dp")),
        check_vma=False,
    )
```

profile of v0, /device:TPU:32, one launch (start us, length us, event | category | flops | bytes accessed | tf_op | source)
XLA Modules:
  0.0 434.9 jit_solution(10324896477999679358)
XLA Ops:
  7.2 2.3 reduce-window.14
  10.1 2.2 reduce-window.16
  12.8 1.5 copy.132
  15.0 2.1 fusion.21
  17.2 1.5 copy.128
  18.7 40.3 %all-gather = f32[32,1,8]{2,1,0:T(1,128)S(1)} all-gather(f32[1,1,8]{2,1,0:T(1,128)S(1)} %copy.98), channel_id=2, replica_groups=mesh['seq'=32,'dp'=8] {'seq'}, dimensions={0}, use_global_device_ids=true | all-gather | bytes 1056 | tf_op jit(solution)/shard_map/all_gather | solution.py:15
  59.1 4.2 multiply_convert_fusion.1
  63.3 1.9 copy-done.1
  65.2 2.8 fusion.27
  68.1 90.6 %all-gather.6.cloned.1.call-done = f32[256,128,128]{2,1,0:T(8,128)} async-done(((f32[8,128,128]{2,1,0:T(8,128)}), f32[256,128,128]{2,1,0:T(8,128)}) %all-gather.6.cloned.1.call-update) | async-done | bytes 16777232 | tf_op jit(solution)/shard_map/all_gather | solution.py:15
  158.6 38.9 %while.20 = (s32[]{:T(128)}, f32[8,128,128]{2,1,0:T(8,128)S(1)}, s32[]{:T(128)}, f32[32,8]{1,0:T(8,128)S(1)}, f32[32,8,128,128]{3,2,1,0:T(8,128)}, /*index=5*/s32[]{:T(128)}, s32[]{:T(128)}) while((s32[]{:T(128)}, f32[8,128,128]{2,1,0:T(8,128)S(1)}, s32[]{:T(128)}, f32[32,8]{1,0:T(8,128)S(1)}, f32[32,8,128,128]{3,2,1,0:T(8,128)}, ...), condition=%wide.region_5.6_spmd.clone, body=%wide.region_4.5_spmd.clone.sunk | while | flops 524292 | bytes 1573073 | solution.py:26
  197.6 4.1 multiply_reduce_fusion
  201.7 14.2 %psum.21 = f32[512]{0:T(512)S(1)} all-reduce(f32[512]{0:T(512)S(1)} %get-tuple-element.452), channel_id=1, replica_groups=mesh['seq'=32,'dp'=8] {'dp'}, use_global_device_ids=true, to_apply=%region_7.8 | all-reduce | flops 512 | bytes 4096 | tf_op jit(solution)/shard_map/psum | solution.py:105
  215.9 3.0 copy.105
  218.8 2.6 fusion.7
  221.4 12.6 %psum.22 = f32[512]{0:T(512)S(1)} all-reduce(f32[512]{0:T(512)S(1)} %get-tuple-element.421), channel_id=1, replica_groups=mesh['seq'=32,'dp'=8] {'dp'}, use_global_device_ids=true, to_apply=%region_9.10 | all-reduce | flops 512 | bytes 4096 | tf_op jit(solution)/shard_map/psum | solution.py:105
  234.0 4.0 fusion.3
  238.0 2.3 copy.129
  240.3 3.2 fusion.24
  243.6 4.2 multiply_convert_fusion
  247.9 1.5 fusion.44
  249.9 2.1 fusion.13
  252.0 2.3 copy.121
  254.3 73.4 %psum.23 = f32[1024]{0:T(1024)} all-reduce(f32[1024]{0:T(1024)S(1)} %get-tuple-element.420), channel_id=1, replica_groups=mesh['seq'=32,'dp'=8] {'seq'}, use_global_device_ids=true, to_apply=%region_13.14 | all-reduce | flops 1024 | bytes 8192 | tf_op jit(solution)/shard_map/psum | solution.py:110
  327.7 4.9 %fusion.45 = f32[8,128,512]{2,1,0:T(8,128)} fusion(bf16[512,8,128]{0,2,1:T(8,128)(2,1)} %bitcast.170, bf16[8,512,512]{2,1,0:T(8,128)(2,1)} %copy-done.1), kind=kOutput, calls=%fused_computation.72 | convolution fusion | flops 536870912 | bytes 7340032 | tf_op jit(solution)/shard_map/while/body/eval_jaxpr/hts,thd->shd/dot_general | solution.py:60
  332.6 2.1 fusion.46
  334.6 44.3 %all-gather.8.cloned.1.call-done = f32[256,128,128]{2,1,0:T(8,128)} async-done(((f32[8,128,128]{2,1,0:T(8,128)}), f32[256,128,128]{2,1,0:T(8,128)}) %all-gather.8.cloned.1.call-update) | async-done | bytes 16777232 | tf_op jit(solution)/shard_map/all_gather | solution.py:15
  378.9 39.3 %while.21 = (s32[]{:T(128)}, f32[8,128,128]{2,1,0:T(8,128)S(1)}, s32[]{:T(128)}, f32[32,8]{1,0:T(8,128)S(1)}, f32[32,8,128,128]{3,2,1,0:T(8,128)}, /*index=5*/s32[]{:T(128)}, s32[]{:T(128)}, s32[]{:T(128)}, s32[]{:T(128)}) while((s32[]{:T(128)}, f32[8,128,128]{2,1,0:T(8,128)S(1)}, s32[]{:T(128)}, f32[32,8]{1,0:T(8,128)S(1)}, ...), condition=%wide.region_11.12_spmd.clone, body=%wide.region_10.11_spmd.clone.sunk | while | flops 524296 | bytes 1573135 | solution.py:26
  418.2 3.7 fusion.9
  421.9 2.3 copy.123
  424.1 2.7 fusion.11
  426.8 1.3 copy.122
  (168 shorter events, 78.6 us)
Async XLA Ops:
  7.2 7.8 %copy-start = (bf16[512,1024]{1,0:T(8,128)(2,1)S(1)}, bf16[512,1024]{1,0:T(8,128)(2,1)}, u32[]{:S(2)}) copy-start(bf16[512,1024]{1,0:T(8,128)(2,1)} %param.12) | copy-start | bytes 3145732
  7.2 151.5 %all-gather.6.cloned.1.call-start = ((), (), s32[]{:S(2)}) async-start(), calls=%async_computation | async-start | bytes 17301504 | tf_op jit(solution)/shard_map/all_gather | solution.py:15
  15.0 2.2 copy-start.5
  17.1 361.9 %all-gather.8.cloned.1.call-start = ((), (), s32[]{:S(2)}) async-start(), calls=%async_computation.1 | async-start | bytes 17301504 | tf_op jit(solution)/shard_map/all_gather | solution.py:15
  63.3 1.9 copy-start.1
  215.9 3.0 copy-start.8
  243.6 4.2 copy-start.6
  247.8 2.0 copy-start.2
  247.8 2.0 copy-start.4
  327.7 4.9 %copy-start.3 = (bf16[8,512,512]{2,1,0:T(8,128)(2,1)S(1)}, bf16[8,512,512]{2,1,0:T(8,128)(2,1)}, u32[]{:S(2)}) copy-start(bf16[8,512,512]{2,1,0:T(8,128)(2,1)} %copy-done.2) | copy-start | bytes 12582916
  378.9 39.3 %copy-start.7 = (bf16[512,1024]{1,0:T(8,128)(2,1)S(1)}, bf16[512,1024]{1,0:T(8,128)(2,1)}, u32[]{:S(2)}) copy-start(bf16[512,1024]{1,0:T(8,128)(2,1)} %param.11) | copy-start | bytes 3145732
Sparse Core Ops, SparseCore 0:
  17.2 141.4 all-gather.5
  243.7 135.2 all-gather.7
where the time goes:
time: 441 us; the launch traced here: 435 us
  blocking collectives  140 us (32%)
  waiting for transfers between devices  135 us (31%)
  other arithmetic  86.9 us (20%)
  matrix products  37.6 us (9%)
  local copies, waits for them, and re-layouts  18.7 us (4%)
  between operations  14.2 us (3%)
    all_gather x2, waiting for transfers between devices, carried_in(): everything = jax.tree.map(lambda part: lax.all_gather(part, axis), x)  135 us
    select_n x64, other arithmetic, hop(): return jax.tree.map(lambda a, b: jnp.where(reached, a, b), new, before)  75.3 us
    psum x1, blocking collectives, on_device(): gain_grad = lax.psum(gain_part, 'seq')  73.4 us
    all_gather x1, blocking collectives, carried_in(): everything = jax.tree.map(lambda part: lax.all_gather(part, axis), x)  40.3 us
    psum x2, blocking collectives, on_device(): squares, gdot = lax.psum((squares, gdot_part), 'dp')  26.7 us
    unnamed x22, local copies, waits for them, and re-layouts  9.85 us
  transfers between devices with their start and end apart: 2, of which 2 were waited for; matrix products, arithmetic and copies ran while one was open for 6% of the time, Pallas kernels for 0%

commit v1 on v0

v1 whole, which is shorter than its diff:
```python
import functools

import jax
import jax.numpy as jnp
from jax import lax
from jax.experimental import pallas as pl
from jax.experimental.pallas import tpu as pltpu
from jax.sharding import PartitionSpec as P

BLOCK = 512
EPSILON = 1e-06
HIGH = lax.Precision.HIGHEST
LANES = 128
GROUP = 2
F32 = jnp.float32
BF16 = jnp.bfloat16
VMEM_LIMIT = 40 * 1024 * 1024


def contract(a, b, dim_a, dim_b, precision=None):
    return lax.dot_general(
        a, b, (((dim_a,), (dim_b,)), ((), ())), precision=precision, preferred_element_type=F32
    )


def halves(x, axis):
    high = x.astype(BF16)
    low = (x - high.astype(F32)).astype(BF16)
    return jnp.concatenate([high, low], axis=axis)


def down(row):
    parts = []
    for at in range(0, row.shape[1], LANES):
        piece = jnp.broadcast_to(row[:, at : at + LANES], (LANES, LANES))
        parts.append(piece.T)
    return jnp.concatenate(parts, axis=0)


def decay_block(column, row, first, edge):
    rows, width = column.shape[0], row.shape[1]
    wide = jnp.concatenate([column] * (width // LANES), axis=1)
    spread = wide - row
    if not edge:
        return jnp.exp(spread)
    place_t = lax.broadcasted_iota(jnp.int32, (rows, width), 0) + first
    place_s = lax.broadcasted_iota(jnp.int32, (rows, width), 1)
    lower = place_t >= place_s
    return jnp.where(lower, jnp.exp(jnp.where(lower, spread, F32(0.0))), F32(0.0))


def state_kernel(a_ref, k_ref, v_ref, cumul_ref, send_ref):
    step = pl.program_id(0)

    @pl.when(step == 0)
    def _():
        place_t = lax.broadcasted_iota(jnp.int32, (LANES, LANES), 0)
        place_s = lax.broadcasted_iota(jnp.int32, (LANES, LANES), 1)
        lower = (place_t >= place_s).astype(F32)
        heads = a_ref.shape[1]
        before = jnp.zeros((1, heads), F32)
        for at in range(0, a_ref.shape[0], LANES):
            piece = contract(lower, a_ref[at : at + LANES, :], 1, 0, HIGH) + before
            before = piece[LANES - 1 :, :]
            wide = jnp.concatenate([piece, jnp.zeros((LANES, LANES - heads), F32)], axis=1)
            cumul_ref[:, at : at + LANES] = wide.T[:heads, :]

    for part in range(GROUP):
        row = cumul_ref[pl.ds(step * GROUP + part, 1), :]
        last = row[:, row.shape[1] - 1 :]
        tail = down(jnp.exp(last - row))
        cols = slice(part * LANES, (part + 1) * LANES)
        k_tail = halves(tail * k_ref[:, cols].astype(F32), 1)
        both = contract(k_tail, v_ref[:, cols], 0, 0)
        update = both[:LANES] + both[LANES:]
        quarters = update.reshape(4, LANES // 4, LANES)
        send_ref[part * 4 : part * 4 + 4, : LANES // 4, :] = quarters
        send_ref[part * 4 : part * 4 + 4, LANES // 4 :, :] = jnp.broadcast_to(
            last.reshape(1, 1, 1), (4, 8, LANES)
        )


def scan_kernel(got_ref, out_ref, through_ref):
    count, rows = out_ref.shape[0], out_ref.shape[1]
    state = jnp.zeros((rows, LANES), F32)
    for at in range(count):
        out_ref[at] = state
        through = jnp.exp(got_ref[at, rows:, :])
        through_ref[at] = through
        state = through[:1] * state + got_ref[at, :rows, :]


def scan_back_kernel(got_ref, through_ref, out_ref):
    count, rows = out_ref.shape[0], LANES // 4
    state = jnp.zeros((rows, LANES), F32)
    gain = jnp.zeros((8, LANES), F32)
    for at in reversed(range(count)):
        out_ref[at, :rows, :] = state
        state = through_ref[at, :1, :] * state + got_ref[at, :rows, :]
        gain = gain + got_ref[at, rows:, :]
    for at in range(count):
        out_ref[at, rows:, :] = gain


def intra_kernel(cumul_ref, q_ref, k_ref, v_ref, probs_ref, intra_ref):
    step = pl.program_id(0)
    tall = 2 * LANES
    for part in range(GROUP):
        row = cumul_ref[pl.ds(step * GROUP + part, 1), :]
        column = down(row)
        cols = slice(part * LANES, (part + 1) * LANES)
        for at in range(0, row.shape[1], tall):
            end = at + tall
            weights = decay_block(column[at:end], row[:, :end], at, True)
            scores = contract(q_ref[at:end, cols], k_ref[:end, cols], 1, 1)
            probs = (weights * scores).astype(BF16)
            probs_ref[part, at:end, :end] = probs
            intra_ref[at:end, cols] = contract(probs, v_ref[:end, cols], 1, 0)


def attn_kernel(cumul_ref, q_ref, state_ref, intra_ref, gain_ref, og_ref, attn_ref, sums_ref, sq_ref, gd_ref):
    step = pl.program_id(0)
    squares = jnp.zeros(sq_ref.shape, F32)
    gdot = jnp.zeros(gd_ref.shape, F32)
    for part in range(GROUP):
        row = cumul_ref[pl.ds(step * GROUP + part, 1), :]
        grow = down(jnp.exp(row))
        cols = slice(part * LANES, (part + 1) * LANES)
        state = halves(state_ref[part], 0)
        q_one = q_ref[:, cols]
        carried = contract(jnp.concatenate([q_one, q_one], axis=1), state, 1, 0)
        attn = intra_ref[:, cols] + grow * carried
        attn_ref[:, cols] = attn
        squares = squares + attn * attn
        gdot = gdot + gain_ref[:, cols] * og_ref[:, cols].astype(F32) * attn

    @pl.when(step == 0)
    def _():
        sq_ref[...] = squares
        gd_ref[...] = gdot

    @pl.when(step > 0)
    def _():
        sq_ref[...] += squares
        gd_ref[...] += gdot

    @pl.when(step == pl.num_programs(0) - 1)
    def _():
        ones = jnp.ones((8, LANES), F32)
        sq_row = contract(ones, sq_ref[...], 1, 1, HIGH)
        gd_row = contract(ones, gd_ref[...], 1, 1, HIGH)
        pieces = [sq_row[:1, at : at + LANES] for at in range(0, BLOCK, LANES)]
        pieces += [gd_row[:1, at : at + LANES] for at in range(0, BLOCK, LANES)]
        whole = jnp.concatenate(pieces, axis=0)
        sums_ref[...] = jnp.broadcast_to(whole[None], sums_ref.shape)


def grad_kernel(
    features, cumul_ref, q_ref, attn_ref, gain_ref, og_ref, sums_ref, normed_ref, grad_ref, send_ref, inv_ref, pull_ref
):
    step = pl.program_id(0)

    @pl.when(step == 0)
    def _():
        whole = jnp.sum(sums_ref[...], axis=0)
        inv_rms = lax.rsqrt(whole[:4] / features + EPSILON)
        pull = inv_rms * inv_rms * inv_rms * whole[4:] / features
        for at in range(4):
            rows = slice(at * LANES, (at + 1) * LANES)
            inv_ref[rows, :] = jnp.broadcast_to(inv_rms[at : at + 1], (LANES, LANES)).T
            pull_ref[rows, :] = jnp.broadcast_to(pull[at : at + 1], (LANES, LANES)).T

    inv_rms, pull = inv_ref[...], pull_ref[...]
    for part in range(GROUP):
        row = cumul_ref[pl.ds(step * GROUP + part, 1), :]
        grow = down(jnp.exp(row))
        cols = slice(part * LANES, (part + 1) * LANES)
        attn, gain = attn_ref[:, cols], gain_ref[:, cols]
        og = og_ref[:, cols].astype(F32)
        scaled = attn * inv_rms
        normed_ref[:, cols] = (scaled * gain).astype(BF16)
        grad = (inv_rms * gain * og - attn * pull).astype(BF16)
        grad_ref[:, cols] = grad
        gain_part = jnp.sum(og * scaled, axis=0, keepdims=True)
        q_grow = halves(grow * q_ref[:, cols].astype(F32), 1)
        both = contract(q_grow, grad, 0, 0)
        update = both[:LANES] + both[LANES:]
        send_ref[part * 4 : part * 4 + 4, : LANES // 4, :] = update.reshape(4, LANES // 4, LANES)
        send_ref[part * 4 : part * 4 + 4, LANES // 4 :, :] = jnp.broadcast_to(
            gain_part[None], (4, 8, LANES)
        )


def intra_back_kernel(
    cumul_ref, q_ref, k_ref, v_ref, grad_ref, probs_ref, state_ref, dq_ref, dk_ref, dv_ref
):
    step = pl.program_id(0)
    tall = 2 * LANES
    for part in range(GROUP):
        row = cumul_ref[pl.ds(step * GROUP + part, 1), :]
        column = down(row)
        grow = down(jnp.exp(row))
        cols = slice(part * LANES, (part + 1) * LANES)
        state = halves(state_ref[part], 1)
        for at in range(0, row.shape[1], tall):
            end = at + tall
            weights = decay_block(column[at:end], row[:, :end], at, True)
            grad = grad_ref[at:end, cols]
            errs = (weights * contract(grad, v_ref[:end, cols], 1, 1)).astype(BF16)
            probs = probs_ref[part, at:end, :end]
            carried = contract(jnp.concatenate([grad, grad], axis=1), state, 1, 1)
            dq = contract(errs, k_ref[:end, cols], 1, 0) + grow[at:end] * carried
            dq_ref[at:end, cols] = dq.astype(BF16)
            dk = contract(errs, q_ref[at:end, cols], 0, 0)
            dv = contract(probs, grad, 0, 0)
            if at:
                dk_ref[:at, cols] += dk[:at]
                dv_ref[:at, cols] += dv[:at]
            dk_ref[at:end, cols] = dk[at:]
            dv_ref[at:end, cols] = dv[at:]


def finish_kernel(cumul_ref, k_ref, v_ref, dk_in_ref, dv_in_ref, flow_ref, dk_ref, dv_ref, gain_ref):
    step = pl.program_id(0)
    for part in range(GROUP):
        row = cumul_ref[pl.ds(step * GROUP + part, 1), :]
        tail = down(jnp.exp(row[:, row.shape[1] - 1 :] - row))
        cols = slice(part * LANES, (part + 1) * LANES)
        flow = flow_ref[part * 4 : part * 4 + 4, : LANES // 4, :].reshape(LANES, LANES)
        k_one, v_one = k_ref[:, cols], v_ref[:, cols]
        dk = contract(jnp.concatenate([v_one, v_one], axis=1), halves(flow, 1), 1, 1)
        dv = contract(jnp.concatenate([k_one, k_one], axis=1), halves(flow, 0), 1, 0)
        dk_ref[:, cols] = (dk_in_ref[:, cols] + tail * dk).astype(BF16)
        dv_ref[:, cols] = (dv_in_ref[:, cols] + tail * dv).astype(BF16)
        gain_ref[:, cols] = flow_ref[part * 4, LANES // 4 : LANES // 4 + 1, :]


def params():
    return pltpu.CompilerParams(dimension_semantics=("arbitrary",), vmem_limit_bytes=VMEM_LIMIT)


def on_device(queries, key_vecs, value_vecs, log_decay, norm_gain, out_grad):
    tokens, wide = queries.shape
    heads = log_decay.shape[1]
    ring = lax.axis_size("seq")
    others = lax.axis_size("dp")
    features = wide * others
    steps = heads // GROUP
    span = GROUP * LANES
    quarter = LANES // 4
    shape = jax.ShapeDtypeStruct
    gain_row = norm_gain.reshape(1, wide)

    columns = pl.BlockSpec((tokens, span), lambda i: (0, i))
    one_row = pl.BlockSpec((1, span), lambda i: (0, i))
    cumul_spec = pl.BlockSpec((heads, tokens), lambda i: (0, 0))
    piece = pl.BlockSpec((GROUP * 4, quarter + 8, LANES), lambda i: (i, 0, 0))
    states = pl.BlockSpec((GROUP, LANES, LANES), lambda i: (i, 0, 0))
    tables = pl.BlockSpec((GROUP, tokens, tokens), lambda i: (i, 0, 0))
    whole_vmem = pl.BlockSpec(memory_space=pltpu.VMEM)

    cumul, send = pl.pallas_call(
        state_kernel,
        grid=(steps,),
        in_specs=[pl.BlockSpec((tokens, heads), lambda i: (0, 0)), columns, columns],
        out_specs=[cumul_spec, piece],
        out_shape=[shape((heads, tokens), F32), shape((ring, quarter + 8, LANES), F32)],
        compiler_params=params(),
        name="state",
    )(log_decay, key_vecs, value_vecs)
    got = lax.all_to_all(send, "seq", 0, 0, tiled=True)
    probs, intra = pl.pallas_call(
        intra_kernel,
        grid=(steps,),
        in_specs=[cumul_spec, columns, columns, columns],
        out_specs=[tables, columns],
        out_shape=[shape((heads, tokens, tokens), BF16), shape((tokens, wide), F32)],
        compiler_params=params(),
        cost_estimate=pl.CostEstimate(
            flops=4 * heads * tokens * tokens * LANES, bytes_accessed=9 * tokens * wide * 2, transcendentals=heads * tokens * tokens
        ),
        name="intra",
    )(cumul, queries, key_vecs, value_vecs)
    before, through = pl.pallas_call(
        scan_kernel,
        in_specs=[whole_vmem],
        out_specs=[whole_vmem, whole_vmem],
        out_shape=[shape((ring, quarter, LANES), F32), shape((ring, 8, LANES), F32)],
        name="scan",
    )(got)
    state_in = lax.all_to_all(before, "seq", 0, 0, tiled=True).reshape(heads, LANES, LANES)
    attn, sums = pl.pallas_call(
        attn_kernel,
        grid=(steps,),
        in_specs=[cumul_spec, columns, states, columns, one_row, columns],
        out_specs=[columns, pl.BlockSpec((others, 8, LANES), lambda i: (0, 0, 0))],
        out_shape=[shape((tokens, wide), F32), shape((others, 8, LANES), F32)],
        scratch_shapes=[pltpu.VMEM((tokens, LANES), F32), pltpu.VMEM((tokens, LANES), F32)],
        compiler_params=params(),
        name="attn",
    )(cumul, queries, state_in, intra, gain_row, out_grad)
    sums = lax.all_to_all(sums, "dp", 0, 0, tiled=True)
    normed, attn_grad, send = pl.pallas_call(
        functools.partial(grad_kernel, features),
        grid=(steps,),
        in_specs=[cumul_spec, columns, columns, one_row, columns, pl.BlockSpec((others, 8, LANES), lambda i: (0, 0, 0))],
        out_specs=[columns, columns, piece],
        out_shape=[shape((tokens, wide), BF16), shape((tokens, wide), BF16), shape((ring, quarter + 8, LANES), F32)],
        scratch_shapes=[pltpu.VMEM((tokens, LANES), F32), pltpu.VMEM((tokens, LANES), F32)],
        compiler_params=params(),
        name="grad",
    )(cumul, queries, attn, gain_row, out_grad, sums)
    got = lax.all_to_all(send, "seq", 0, 0, tiled=True)
    dq, dk, dv = pl.pallas_call(
        intra_back_kernel,
        grid=(steps,),
        in_specs=[cumul_spec, columns, columns, columns, columns, tables, states],
        out_specs=[columns, columns, columns],
        out_shape=[shape((tokens, wide), BF16), shape((tokens, wide), F32), shape((tokens, wide), F32)],
        compiler_params=params(),
        cost_estimate=pl.CostEstimate(
            flops=8 * heads * tokens * tokens * LANES, bytes_accessed=14 * tokens * wide * 2, transcendentals=heads * tokens * tokens
        ),
        name="intra_back",
    )(cumul, queries, key_vecs, value_vecs, attn_grad, probs, state_in)
    after = pl.pallas_call(
        scan_back_kernel,
        in_specs=[whole_vmem, whole_vmem],
        out_specs=whole_vmem,
        out_shape=shape((ring, quarter + 8, LANES), F32),
        name="scan_back",
    )(got, through)
    flow = lax.all_to_all(after, "seq", 0, 0, tiled=True)
    dk, dv, gain_grad = pl.pallas_call(
        finish_kernel,
        grid=(steps,),
        in_specs=[cumul_spec, columns, columns, columns, columns, piece],
        out_specs=[columns, columns, one_row],
        out_shape=[shape((tokens, wide), BF16), shape((tokens, wide), BF16), shape((1, wide), F32)],
        compiler_params=params(),
        name="finish",
    )(cumul, key_vecs, value_vecs, dk, dv, flow)
    return normed, dq, dk, dv, gain_grad.reshape(wide)


def solution(mesh):
    placed = (
        P("seq", "dp"),
        P("seq", "dp"),
        P("seq", "dp"),
        P("seq", "dp"),
        P("dp"),
        P("seq", "dp"),
    )
    return jax.shard_map(
        on_device,
        mesh=mesh,
        in_specs=placed,
        out_specs=(P("seq", "dp"), P("seq", "dp"), P("seq", "dp"), P("seq", "dp"), P("dp")),
        check_vma=False,
    )
```

time: 441 us -> 145 us (0.33); the launches traced: 435 us -> 144 us
  waiting for transfers between devices: 135 us -> 14.8 us
  other arithmetic: 86.9 us -> 0 us
  blocking collectives: 140 us -> 66.2 us
  matrix products: 37.6 us -> 0 us
  Pallas kernels: 0 us -> 32.2 us
  between operations: 14.2 us -> 0.77 us
  starting transfers between devices: 0.08 us -> 10.1 us
    all_gather x2 -> x0, waiting for transfers between devices: 135 us -> none  [carried_in(): everything = jax.tree.map(lambda part: lax.all_gather(part, axis), x)]
    psum x3 -> x0, blocking collectives: 100 us -> none  [the longest x1 73.4 us: on_device(): gain_grad = lax.psum(gain_part, 'seq')]
    select_n x64 -> x0, other arithmetic: 75.3 us -> none  [hop(): return jax.tree.map(lambda a, b: jnp.where(reached, a, b), new, before)]
    all_to_all x0 -> x3, blocking collectives: none -> 66.2 us  [the longest x2 56.6 us: on_device(): got = lax.all_to_all(send, 'seq', 0, 0, tiled=True)]
    all_gather x1 -> x0, blocking collectives: 40.3 us -> none  [carried_in(): everything = jax.tree.map(lambda part: lax.all_gather(part, axis), x)]
    dot_general x12 -> x0, matrix products: 37.6 us -> none  [the longest x1 4.89 us: intra_backward(): jnp.einsum('hts,thd->shd', probs, g_blk, preferred_element_type=jnp.float32)]
    pallas_call x0 -> x8, Pallas kernels: none -> 32.2 us  [the longest x1 8.5 us: on_device(): pl.pallas_call(intra_back_kernel, grid=(steps,), in_specs=[cumul_spec, co...]
    all_to_all x0 -> x2, waiting for transfers between devices: none -> 14.8 us  [the longest x1 9.55 us: on_device(): lax.all_to_all(before, 'seq', 0, 0, tiled=True).reshape(heads, LANES, LANES)]
  transfers between devices with their start and end apart: 2 -> 2, of which waited for: 2 -> 2; matrix products, arithmetic and copies ran while one was open for 6% -> 0% of each run, Pallas kernels for 0% -> 9%
where the time goes in v1:
time: 145 us; the launch traced here: 144 us
  blocking collectives  66.2 us (46%)
  Pallas kernels  32.2 us (22%)
  local copies, waits for them, and re-layouts  19.6 us (14%)
  waiting for transfers between devices  14.8 us (10%)
  starting transfers between devices  10.1 us (7%)
    all_to_all x2, blocking collectives, on_device(): got = lax.all_to_all(send, 'seq', 0, 0, tiled=True)  56.6 us
    unnamed x35, local copies, waits for them, and re-layouts  19.6 us
    all_to_all x1, waiting for transfers between devices, on_device(): lax.all_to_all(before, 'seq', 0, 0, tiled=True).reshape(heads, LANES, LANES)  9.55 us
    all_to_all x1, blocking collectives, on_device(): sums = lax.all_to_all(sums, 'dp', 0, 0, tiled=True)  9.55 us
    pallas_call x1, Pallas kernels, on_device(): pl.pallas_call(intra_back_kernel, grid=(steps,), in_specs=[cumul_spec, co...  8.5 us
    all_to_all x1, waiting for transfers between devices, on_device(): flow = lax.all_to_all(after, 'seq', 0, 0, tiled=True)  5.28 us
    all_to_all x1, starting transfers between devices, on_device(): lax.all_to_all(before, 'seq', 0, 0, tiled=True).reshape(heads, LANES, LANES)  5.08 us
    all_to_all x1, starting transfers between devices, on_device(): flow = lax.all_to_all(after, 'seq', 0, 0, tiled=True)  5.07 us
  transfers between devices with their start and end apart: 2, of which 2 were waited for; matrix products, arithmetic and copies ran while one was open for 0% of the time, Pallas kernels for 9%

profile of v1, /device:TPU:32, one launch (start us, length us, event | category | flops | bytes accessed | tf_op | source)
XLA Modules:
  0.0 143.7 jit_solution(1533438824882188666)
XLA Ops:
  0.6 0.8 copy.11.a_ref
  1.5 0.0 copy-start.1
  1.5 1.2 copy-done.1
  2.7 1.2 copy-done.3
  3.9 3.3 %state.1 = (f32[8,512]{1,0:T(8,128)S(1)}, f32[32,40,128]{2,1,0:T(8,128)S(1)}) custom-call(f32[512,8]{1,0:T(8,128)S(1)} %copy.11.a_ref, bf16[512,1024]{1,0:T(8,128)(2,1)S(1)} %copy-done.1, bf16[512,1024]{1,0:T(8,128)(2,1)S(1)} %copy-done.3), custom_call_target="tpu_custom_call" | custom-call | tf_op jit(solution)/shard_map/state/pallas_call | solution.py:262
  7.2 0.0 copy-start
  7.2 31.6 %all_to_all.25.got_ref = f32[32,40,128]{2,1,0:T(8,128)} all-to-all(f32[32,40,128]{2,1,0:T(8,128)S(1)} %get-tuple-element.23), channel_id=1, replica_groups=mesh['seq'=32,'dp'=8] {'seq'}, dimensions={0} | all-to-all | bytes 1310720 | tf_op jit(solution)/shard_map/all_to_all | solution.py:271
  38.9 2.0 %scan.1 = (f32[32,32,128]{2,1,0:T(8,128)}, f32[32,8,128]{2,1,0:T(8,128)}) custom-call(f32[32,40,128]{2,1,0:T(8,128)} %all_to_all.25.got_ref), custom_call_target="tpu_custom_call" | custom-call | tf_op jit(solution)/shard_map/scan/pallas_call | solution.py:284
  40.8 5.1 %all-to-all-start.1 = ((f32[32,32,128]{2,1,0:T(8,128)}), f32[32,32,128]{2,1,0:T(8,128)}, u32[]{:S(2)}, u32[]{:S(2)}) async-start(f32[32,32,128]{2,1,0:T(8,128)} %get-tuple-element.24), calls=%async_computation.1 | async-start | bytes 1048576 | tf_op jit(solution)/shard_map/all_to_all | solution.py:291
  45.9 0.0 copy-start.16
  46.0 4.3 %intra.1 = (bf16[8,512,512]{2,1,0:T(8,128)(2,1)S(1)}, f32[512,1024]{1,0:T(8,128)S(1)}) custom-call(f32[8,512]{1,0:T(8,128)S(1)} %get-tuple-element.22.cumul_ref, bf16[512,1024]{1,0:T(8,128)(2,1)S(1)} %copy-done, bf16[512,1024]{1,0:T(8,128)(2,1)S(1)} %copy-done.2, bf16[512,1024]{1,0:T(8,128)(2,1)S(1)} %copy-done.4), custom_call_target="tpu_custom_call" | custom-call | flops 1073741824 | bytes 9437184 | tf_op jit(solution)/shard_map/intra/pallas_call | solution.py:272
  50.3 1.9 %copy-done.5 = bf16[8,512,512]{2,1,0:T(8,128)(2,1)} copy-done((bf16[8,512,512]{2,1,0:T(8,128)(2,1)}, bf16[8,512,512]{2,1,0:T(8,128)(2,1)S(1)}, u32[]{:S(2)}) %copy-start.5) | copy-done | bytes 4194328
  52.2 1.4 copy-done.12
  53.6 9.5 %all-to-all-done.1 = f32[32,32,128]{2,1,0:T(8,128)} async-done(((f32[32,32,128]{2,1,0:T(8,128)}), f32[32,32,128]{2,1,0:T(8,128)}, u32[]{:S(2)}, u32[]{:S(2)}) %all-to-all-start.1) | async-done | bytes 524320 | tf_op jit(solution)/shard_map/all_to_all | solution.py:291
  63.1 1.2 copy-done.7
  64.3 1.6 %copy-done.13 = f32[512,1024]{1,0:T(8,128)S(1)} copy-done((f32[512,1024]{1,0:T(8,128)S(1)}, f32[512,1024]{1,0:T(8,128)}, u32[]{:S(2)}) %copy-start.13) | copy-done | bytes 2097176
  65.9 3.7 %attn.1 = (f32[512,1024]{1,0:T(8,128)S(1)}, f32[8,8,128]{2,1,0:T(8,128)S(1)}) custom-call(f32[8,512]{1,0:T(8,128)S(1)} %get-tuple-element.22.cumul_ref, bf16[512,1024]{1,0:T(8,128)(2,1)S(1)} %copy-done, f32[8,128,128]{2,1,0:T(8,128)} %bitcast.state_ref, f32[512,1024]{1,0:T(8,128)S(1)} %copy-done.13, f32[1,1024]{1,0:T(1,128)S(1)} %bitcast.3, ...), custom_call_target="tpu_custom_call" | custom-call | tf_op jit(solution)/shard_map/attn/pallas_call | solution.py:292
  69.7 9.5 %all_to_all.26.sums_ref = f32[8,8,128]{2,1,0:T(8,128)S(1)} all-to-all(f32[8,8,128]{2,1,0:T(8,128)S(1)} %get-tuple-element.27), channel_id=1, replica_groups=mesh['seq'=32,'dp'=8] {'dp'}, dimensions={0} | all-to-all | bytes 65536 | tf_op jit(solution)/shard_map/all_to_all | solution.py:302
  79.2 3.8 %grad.1 = (bf16[512,1024]{1,0:T(8,128)(2,1)}, bf16[512,1024]{1,0:T(8,128)(2,1)S(1)}, f32[32,40,128]{2,1,0:T(8,128)S(1)}) custom-call(f32[8,512]{1,0:T(8,128)S(1)} %get-tuple-element.22.cumul_ref, bf16[512,1024]{1,0:T(8,128)(2,1)S(1)} %copy-done, f32[512,1024]{1,0:T(8,128)S(1)} %get-tuple-element.26.attn_ref, f32[1,1024]{1,0:T(1,128)S(1)} %bitcast.4, ...), custom_call_target="tpu_custom_call" | custom-call | tf_op jit(solution)/shard_map/grad/pallas_call | solution.py:303
  83.0 1.0 copy-done.14
  84.0 25.0 %all_to_all.27.got_ref = f32[32,40,128]{2,1,0:T(8,128)} all-to-all(f32[32,40,128]{2,1,0:T(8,128)S(1)} %get-tuple-element.34), channel_id=1, replica_groups=mesh['seq'=32,'dp'=8] {'seq'}, dimensions={0} | all-to-all | bytes 1310720 | tf_op jit(solution)/shard_map/all_to_all | solution.py:313
  108.9 2.0 %scan_back.1 = f32[32,40,128]{2,1,0:T(8,128)} custom-call(f32[32,40,128]{2,1,0:T(8,128)} %all_to_all.27.got_ref, f32[32,8,128]{2,1,0:T(8,128)} %get-tuple-element.35.through_ref), custom_call_target="tpu_custom_call" | custom-call | tf_op jit(solution)/shard_map/scan_back/pallas_call | solution.py:326
  110.9 5.1 %all-to-all-start.4 = ((f32[32,40,128]{2,1,0:T(8,128)}), f32[32,40,128]{2,1,0:T(8,128)}, u32[]{:S(2)}, u32[]{:S(2)}) async-start(f32[32,40,128]{2,1,0:T(8,128)} %scan_back.1), calls=%async_computation.4 | async-start | bytes 1310720 | tf_op jit(solution)/shard_map/all_to_all | solution.py:333
  116.0 2.2 %copy-done.6 = bf16[8,512,512]{2,1,0:T(8,128)(2,1)S(1)} copy-done((bf16[8,512,512]{2,1,0:T(8,128)(2,1)S(1)}, bf16[8,512,512]{2,1,0:T(8,128)(2,1)}, u32[]{:S(2)}) %copy-start.6) | copy-done | bytes 4194328
  118.2 1.2 copy-done.15
  119.4 8.5 %intra_back.1 = (bf16[512,1024]{1,0:T(8,128)(2,1)}, f32[512,1024]{1,0:T(8,128)S(1)}, f32[512,1024]{1,0:T(8,128)S(1)}) custom-call(f32[8,512]{1,0:T(8,128)S(1)} %get-tuple-element.22.cumul_ref, bf16[512,1024]{1,0:T(8,128)(2,1)S(1)} %copy-done, bf16[512,1024]{1,0:T(8,128)(2,1)S(1)} %copy-done.2, bf16[512,1024]{1,0:T(8,128)(2,1)S(1)} %copy-done.4, ...), custom_call_target="tpu_custom_call" | custom-call | flops 2147483648 | bytes 14680064 | tf_op jit(solution)/shard_map/intra_back/pallas_call | solution.py:314
  127.9 1.3 copy-done.8
  129.3 1.3 copy-done.10
  130.6 5.3 %all-to-all-done.4.flow_ref = f32[32,40,128]{2,1,0:T(8,128)} async-done(((f32[32,40,128]{2,1,0:T(8,128)}), f32[32,40,128]{2,1,0:T(8,128)}, u32[]{:S(2)}, u32[]{:S(2)}) %all-to-all-start.4) | async-done | bytes 655392 | tf_op jit(solution)/shard_map/all_to_all | solution.py:333
  135.8 1.6 %copy-done.9 = f32[512,1024]{1,0:T(8,128)S(1)} copy-done((f32[512,1024]{1,0:T(8,128)S(1)}, f32[512,1024]{1,0:T(8,128)}, u32[]{:S(2)}) %copy-start.9) | copy-done | bytes 2097176
  137.4 1.6 %copy-done.11 = f32[512,1024]{1,0:T(8,128)S(1)} copy-done((f32[512,1024]{1,0:T(8,128)S(1)}, f32[512,1024]{1,0:T(8,128)}, u32[]{:S(2)}) %copy-start.11) | copy-done | bytes 2097176
  139.0 4.6 %finish.1 = (bf16[512,1024]{1,0:T(8,128)(2,1)}, bf16[512,1024]{1,0:T(8,128)(2,1)}, f32[1,1024]{1,0:T(1,128)}) custom-call(f32[8,512]{1,0:T(8,128)S(1)} %get-tuple-element.22.cumul_ref, bf16[512,1024]{1,0:T(8,128)(2,1)S(1)} %copy-done.2, bf16[512,1024]{1,0:T(8,128)(2,1)S(1)} %copy-done.4, f32[512,1024]{1,0:T(8,128)S(1)} %copy-done.9, ...), custom_call_target="tpu_custom_call" | custom-call | tf_op jit(solution)/shard_map/finish/pallas_call | solution.py:334
  (18 shorter events, 0.0 us)
Async XLA Ops:
  1.5 1.2 copy-start.1
  2.7 1.2 copy-start.3
  3.9 42.0 %copy-start.4 = (bf16[512,1024]{1,0:T(8,128)(2,1)S(1)}, bf16[512,1024]{1,0:T(8,128)(2,1)}, u32[]{:S(2)}) copy-start(bf16[512,1024]{1,0:T(8,128)(2,1)} %v_ref.7) | copy-start | bytes 3145732
  7.2 38.7 %copy-start = (bf16[512,1024]{1,0:T(8,128)(2,1)S(1)}, bf16[512,1024]{1,0:T(8,128)(2,1)}, u32[]{:S(2)}) copy-start(bf16[512,1024]{1,0:T(8,128)(2,1)} %q_ref.7) | copy-start | bytes 3145732
  7.2 38.7 %copy-start.2 = (bf16[512,1024]{1,0:T(8,128)(2,1)S(1)}, bf16[512,1024]{1,0:T(8,128)(2,1)}, u32[]{:S(2)}) copy-start(bf16[512,1024]{1,0:T(8,128)(2,1)} %k_ref.7) | copy-start | bytes 3145732
  40.8 22.3 %all-to-all-start.1 = ((f32[32,32,128]{2,1,0:T(8,128)}), f32[32,32,128]{2,1,0:T(8,128)}, u32[]{:S(2)}, u32[]{:S(2)}) async-start(f32[32,32,128]{2,1,0:T(8,128)} %get-tuple-element.24), calls=%async_computation.1 | async-start | bytes 1048576 | tf_op jit(solution)/shard_map/all_to_all | solution.py:291
  45.9 17.2 %copy-start.16 = (f32[1024]{0:T(1024)S(1)}, f32[1024]{0:T(1024)}, u32[]{:S(2)}) copy-start(f32[1024]{0:T(1024)} %param.10) | copy-start | bytes 12292
  50.3 2.0 %copy-start.5 = (bf16[8,512,512]{2,1,0:T(8,128)(2,1)}, bf16[8,512,512]{2,1,0:T(8,128)(2,1)S(1)}, u32[]{:S(2)}) copy-start(bf16[8,512,512]{2,1,0:T(8,128)(2,1)S(1)} %get-tuple-element.30.probs_ref) | copy-start | bytes 12582916
  52.2 1.4 copy-start.12
  63.1 1.2 copy-start.7
  64.3 1.6 %copy-start.13 = (f32[512,1024]{1,0:T(8,128)S(1)}, f32[512,1024]{1,0:T(8,128)}, u32[]{:S(2)}) copy-start(f32[512,1024]{1,0:T(8,128)} %copy-done.12) | copy-start | bytes 6291460
  83.0 1.0 copy-start.14
  110.9 24.9 %all-to-all-start.4 = ((f32[32,40,128]{2,1,0:T(8,128)}), f32[32,40,128]{2,1,0:T(8,128)}, u32[]{:S(2)}, u32[]{:S(2)}) async-start(f32[32,40,128]{2,1,0:T(8,128)} %scan_back.1), calls=%async_computation.4 | async-start | bytes 1310720 | tf_op jit(solution)/shard_map/all_to_all | solution.py:333
  116.0 2.2 %copy-start.6 = (bf16[8,512,512]{2,1,0:T(8,128)(2,1)S(1)}, bf16[8,512,512]{2,1,0:T(8,128)(2,1)}, u32[]{:S(2)}) copy-start(bf16[8,512,512]{2,1,0:T(8,128)(2,1)} %copy-done.5) | copy-start | bytes 12582916
  118.2 1.2 copy-start.15
  127.9 1.3 copy-start.8
  129.3 1.3 copy-start.10
  135.8 1.6 %copy-start.9 = (f32[512,1024]{1,0:T(8,128)S(1)}, f32[512,1024]{1,0:T(8,128)}, u32[]{:S(2)}) copy-start(f32[512,1024]{1,0:T(8,128)} %copy-done.8) | copy-start | bytes 6291460
  137.4 1.6 %copy-start.11 = (f32[512,1024]{1,0:T(8,128)S(1)}, f32[512,1024]{1,0:T(8,128)}, u32[]{:S(2)}) copy-start(f32[512,1024]{1,0:T(8,128)} %copy-done.10) | copy-start | bytes 6291460

commit v2 on v0

v2 whole, which is shorter than its diff:
```python
import functools

import jax
import jax.numpy as jnp
from jax import lax
from jax.experimental import pallas as pl
from jax.experimental.pallas import tpu as pltpu
from jax.sharding import PartitionSpec as P

BLOCK = 512
EPSILON = 1e-06
HIGH = lax.Precision.HIGHEST
LANES = 128
GROUP = 2
QUARTER = LANES // 4
PIECE = QUARTER + 1
F32 = jnp.float32
BF16 = jnp.bfloat16
VMEM_LIMIT = 12 * 1024 * 1024


def contract(a, b, dim_a, dim_b, precision=None):
    return lax.dot_general(
        a, b, (((dim_a,), (dim_b,)), ((), ())), precision=precision, preferred_element_type=F32
    )


def halves(x, axis):
    high = x.astype(BF16)
    low = (x - high.astype(F32)).astype(BF16)
    return jnp.concatenate([high, low], axis=axis)


def down(row):
    parts = []
    for at in range(0, row.shape[1], LANES):
        piece = jnp.broadcast_to(row[:, at : at + LANES], (LANES, LANES))
        parts.append(piece.T)
    return jnp.concatenate(parts, axis=0)


def decay_block(column, row, first, edge):
    rows, width = column.shape[0], row.shape[1]
    wide = jnp.concatenate([column] * (width // LANES), axis=1)
    spread = wide - row
    if not edge:
        return jnp.exp(spread)
    place_t = lax.broadcasted_iota(jnp.int32, (rows, width), 0) + first
    place_s = lax.broadcasted_iota(jnp.int32, (rows, width), 1)
    return jnp.where(place_t >= place_s, jnp.exp(spread), F32(0.0))


def cols(head, count=1):
    return slice(head * LANES, (head + count) * LANES)


def pack(send_ref, head, update, extra):
    for quarter in range(4):
        first = (head * 4 + quarter) * PIECE
        send_ref[first : first + QUARTER, :] = update[quarter * QUARTER : (quarter + 1) * QUARTER]
        send_ref[first + QUARTER : first + PIECE, :] = extra


def copies_of(pairs, heads, sems):
    every = []
    for at in range(0, heads, GROUP):
        here = (slice(None), cols(at, GROUP))
        for which, (src, dst) in enumerate(pairs):
            every.append(pltpu.make_async_copy(src.at[here], dst.at[here], sems.at[which, at // GROUP]))
    return every


def on_turn(body, turn):
    def kernel(core_ref, *refs):
        @pl.when(core_ref[0] == turn)
        def _():
            body(*refs)

    return kernel


def front_kernel(a_hbm, k_hbm, v_hbm, cumul_ref, send_ref, k_ref, v_ref, a_ref, a_sem, sems):
    heads, tokens = a_ref.shape
    a_copy = pltpu.make_async_copy(a_hbm, a_ref, a_sem)
    a_copy.start()
    early = copies_of(((k_hbm, k_ref), (v_hbm, v_ref)), heads, sems)
    for copy in early:
        copy.start()
    place_s = lax.broadcasted_iota(jnp.int32, (LANES, LANES), 0)
    place_t = lax.broadcasted_iota(jnp.int32, (LANES, LANES), 1)
    upper = (place_s <= place_t).astype(F32)
    before = jnp.zeros((heads, 1), F32)
    a_copy.wait()
    for at in range(0, tokens, LANES):
        piece = contract(a_ref[:, at : at + LANES], upper, 1, 0, HIGH) + before
        before = piece[:, LANES - 1 :]
        cumul_ref[:, at : at + LANES] = piece
    for head in range(heads):
        if head % GROUP == 0:
            for copy in early[:2]:
                copy.wait()
            early = early[2:]
        row = cumul_ref[head : head + 1, :]
        last = row[:, tokens - 1 :]
        k_tail = k_ref[:, cols(head)].T.astype(F32) * jnp.exp(last - row)
        both = contract(halves(k_tail, 0), v_ref[:, cols(head)], 1, 0)
        pack(send_ref, head, both[:LANES] + both[LANES:], jnp.broadcast_to(last, (1, LANES)))


def scan_kernel(got_ref, out_ref, through_ref):
    count = out_ref.shape[0]
    state = jnp.zeros((QUARTER, LANES), F32)
    for at in range(count):
        out_ref[at] = state
        first = at * PIECE
        through = jnp.exp(got_ref[first + QUARTER : first + PIECE, :])
        through_ref[at : at + 1, :] = through
        state = through * state + got_ref[first : first + QUARTER, :]


def scan_back_kernel(got_ref, through_ref, out_ref):
    count = through_ref.shape[0]
    state = jnp.zeros((QUARTER, LANES), F32)
    gain = jnp.zeros((1, LANES), F32)
    for at in reversed(range(count)):
        first = at * PIECE
        out_ref[first : first + QUARTER, :] = state
        state = through_ref[at : at + 1, :] * state + got_ref[first : first + QUARTER, :]
        gain = gain + got_ref[first + QUARTER : first + PIECE, :]
    for at in range(count):
        out_ref[at * PIECE + QUARTER : (at + 1) * PIECE, :] = gain


def intra_kernel(
    cumul_ref, q_hbm, og_hbm, k_ref, v_ref, probs_ref, intra_ref, grow_ref, tail_ref, pull_ref, q_ref, og_ref, sems
):
    heads, tokens = cumul_ref.shape
    tall = 2 * LANES
    copies = copies_of(((q_hbm, q_ref), (og_hbm, og_ref)), heads, sems)
    for copy in copies[0::2] + copies[1::2]:
        copy.start()
    for head in range(heads):
        if head % GROUP == 0:
            copies[head // GROUP * 2].wait()
        row = cumul_ref[head : head + 1, :]
        last = row[:, tokens - 1 :]
        column = down(row)
        mine = cols(head)
        grow_ref[:, mine] = jnp.exp(column)
        tail_ref[:, mine] = jnp.exp(last - column)
        pull_ref[head] = halves(q_ref[:, mine].T.astype(F32) * jnp.exp(row), 0)
        for at in range(0, tokens, tall):
            end = at + tall
            weights = decay_block(column[at:end], row[:, :end], at, True)
            scores = contract(q_ref[at:end, mine], k_ref[:end, mine], 1, 1)
            probs = (weights * scores).astype(BF16)
            probs_ref[head, at:end, :end] = probs
            intra_ref[at:end, mine] = contract(probs, v_ref[:end, mine], 1, 0)
    for copy in copies[1::2]:
        copy.wait()


def attn_kernel(q_ref, state_ref, intra_ref, grow_ref, gain_ref, og_ref, attn_ref, sums_ref, sq_ref, gd_ref):
    for at in range(0, state_ref.shape[0], GROUP):
        squares = jnp.zeros(sq_ref.shape, F32) if at == 0 else sq_ref[...]
        gdot = jnp.zeros(gd_ref.shape, F32) if at == 0 else gd_ref[...]
        for head in range(at, at + GROUP):
            mine = cols(head)
            q_one = q_ref[:, mine]
            carried = contract(jnp.concatenate([q_one, q_one], axis=1), halves(state_ref[head], 0), 1, 0)
            attn = intra_ref[:, mine] + grow_ref[:, mine] * carried
            attn_ref[:, mine] = attn
            squares = squares + attn * attn
            gdot = gdot + gain_ref[:, mine] * og_ref[:, mine].astype(F32) * attn
        sq_ref[...] = squares
        gd_ref[...] = gdot
    ones = jnp.ones((8, LANES), F32)
    sq_row = contract(ones, sq_ref[...], 1, 1, HIGH)
    gd_row = contract(ones, gd_ref[...], 1, 1, HIGH)
    pieces = [sq_row[:1, at : at + LANES] for at in range(0, BLOCK, LANES)]
    pieces += [gd_row[:1, at : at + LANES] for at in range(0, BLOCK, LANES)]
    whole = jnp.concatenate(pieces, axis=0)
    sums_ref[...] = jnp.broadcast_to(whole[None], sums_ref.shape)


def grad_kernel(features, pull_ref, attn_ref, gain_ref, og_ref, sums_ref, grad_ref, send_ref, inv_ref, back_ref):
    whole = jnp.sum(sums_ref[...], axis=0)
    inv_rms = lax.rsqrt(whole[:4] / features + EPSILON)
    back = inv_rms * inv_rms * inv_rms * whole[4:] / features
    for at in range(4):
        inv_ref[cols(at), :] = jnp.broadcast_to(inv_rms[at : at + 1], (LANES, LANES)).T
        back_ref[cols(at), :] = jnp.broadcast_to(back[at : at + 1], (LANES, LANES)).T
    for head in range(pull_ref.shape[0]):
        mine = cols(head)
        og = og_ref[:, mine].astype(F32)
        grad = inv_ref[...] * gain_ref[:, mine] * og - attn_ref[:, mine] * back_ref[...]
        grad = grad.astype(BF16)
        grad_ref[:, mine] = grad
        both = contract(pull_ref[head], grad, 1, 0)
        update = both[:LANES] + both[LANES:]
        gain_part = jnp.sum(og * (attn_ref[:, mine] * inv_ref[...]), axis=0, keepdims=True)
        pack(send_ref, head, update, gain_part)


def intra_back_kernel(
    cumul_ref, q_ref, k_ref, v_ref, grad_ref, probs_ref, state_ref, grow_ref, attn_ref, gain_ref, inv_ref,
    dq_hbm, normed_hbm, dk_ref, dv_ref, dq_ref, normed_ref, sems,
):
    heads, tokens = cumul_ref.shape
    tall = 2 * LANES
    copies = []
    for head in range(heads):
        row = cumul_ref[head : head + 1, :]
        column = down(row)
        mine = cols(head)
        scaled = attn_ref[:, mine] * inv_ref[...]
        normed_ref[:, mine] = (scaled * gain_ref[:, mine]).astype(BF16)
        state = halves(state_ref[head], 1)
        for at in range(0, tokens, tall):
            end = at + tall
            weights = decay_block(column[at:end], row[:, :end], at, True)
            grad = grad_ref[at:end, mine]
            errs = (weights * contract(grad, v_ref[:end, mine], 1, 1)).astype(BF16)
            probs = probs_ref[head, at:end, :end]
            carried = contract(jnp.concatenate([grad, grad], axis=1), state, 1, 1)
            dq = contract(errs, k_ref[:end, mine], 1, 0) + grow_ref[at:end, mine] * carried
            dq_ref[at:end, mine] = dq.astype(BF16)
            dk = contract(errs, q_ref[at:end, mine], 0, 0)
            dv = contract(probs, grad, 0, 0)
            if at:
                dk_ref[:at, mine] += dk[:at]
                dv_ref[:at, mine] += dv[:at]
            dk_ref[at:end, mine] = dk[at:]
            dv_ref[at:end, mine] = dv[at:]
        if head % GROUP == GROUP - 1:
            here = (slice(None), cols(head + 1 - GROUP, GROUP))
            for which, (src, dst) in enumerate(((dq_ref, dq_hbm), (normed_ref, normed_hbm))):
                copy = pltpu.make_async_copy(src.at[here], dst.at[here], sems.at[which, head // GROUP])
                copy.start()
                copies.append(copy)
    for copy in copies:
        copy.wait()


def finish_kernel(k_ref, v_ref, dk_in_ref, dv_in_ref, tail_ref, flow_ref, dk_hbm, dv_hbm, gain_ref, dk_ref, dv_ref, sems):
    copies = []
    for head in range(gain_ref.shape[0]):
        mine = cols(head)
        firsts = [(head * 4 + quarter) * PIECE for quarter in range(4)]
        flow = jnp.concatenate([flow_ref[first : first + QUARTER, :] for first in firsts], axis=0)
        gain_ref[head : head + 1, :] = flow_ref[firsts[0] + QUARTER : firsts[0] + PIECE, :]
        k_one, v_one = k_ref[:, mine], v_ref[:, mine]
        dk = contract(jnp.concatenate([v_one, v_one], axis=1), halves(flow, 1), 1, 1)
        dv = contract(jnp.concatenate([k_one, k_one], axis=1), halves(flow, 0), 1, 0)
        tail = tail_ref[:, mine]
        dk_ref[:, mine] = (dk_in_ref[:, mine] + tail * dk).astype(BF16)
        dv_ref[:, mine] = (dv_in_ref[:, mine] + tail * dv).astype(BF16)
        if head % GROUP == GROUP - 1:
            here = (slice(None), cols(head + 1 - GROUP, GROUP))
            for which, (src, dst) in enumerate(((dk_ref, dk_hbm), (dv_ref, dv_hbm))):
                copy = pltpu.make_async_copy(src.at[here], dst.at[here], sems.at[which, head // GROUP])
                copy.start()
                copies.append(copy)
    for copy in copies:
        copy.wait()


def call(kernel, name, ins, outs, scratch=(), into=None):
    place = lambda space: pl.BlockSpec(memory_space=space)
    pin = lambda array, space: pltpu.with_memory_space_constraint(array, space) if space == pltpu.HBM else array
    spaces = [space for _, space in ins]
    arrays = [pin(array, space) for array, space in ins]
    aliases = {}
    body = kernel
    if into is not None:
        known, count = len(ins), len(outs)
        aliases = {known + at: at for at in range(count)}
        spaces += [space for _, _, space in outs]
        arrays += [pin(array, space) for array, (_, _, space) in zip(into, outs)]
        body = lambda *refs: kernel(*refs[:known], *refs[known + count :])
    return pl.pallas_call(
        body,
        in_specs=[place(space) for space in spaces],
        out_specs=[place(space) for _, _, space in outs],
        out_shape=[jax.ShapeDtypeStruct(shape, dtype) for shape, dtype, _ in outs],
        scratch_shapes=list(scratch),
        input_output_aliases=aliases,
        compiler_params=pltpu.CompilerParams(vmem_limit_bytes=VMEM_LIMIT),
        name=name,
    )(*arrays)


def exchange(x):
    return lax.all_to_all(x.reshape(-1), "seq", 0, 0, tiled=True).reshape(x.shape)


def on_device(queries, key_vecs, value_vecs, log_decay, norm_gain, out_grad):
    tokens, wide = queries.shape
    heads = log_decay.shape[1]
    ring = lax.axis_size("seq")
    others = lax.axis_size("dp")
    features = wide * others
    groups = heads // GROUP
    gain_row = norm_gain.reshape(1, wide)
    vm, hbm = pltpu.VMEM, pltpu.HBM
    core = (lax.axis_index("dp") & 1).astype(jnp.int32).reshape(1)
    turn = (core, pltpu.SMEM)
    flat = (tokens, wide)
    pieces = (ring, QUARTER, LANES)
    packed = (ring * PIECE, LANES)
    both_sems = pltpu.SemaphoreType.DMA((2, groups))

    cumul, send, k, v = call(
        front_kernel,
        "front",
        [(log_decay.T, hbm), (key_vecs, hbm), (value_vecs, hbm)],
        [((heads, tokens), F32, vm), (packed, F32, vm)] + [(flat, BF16, vm)] * 2,
        [pltpu.VMEM((heads, tokens), F32), pltpu.SemaphoreType.DMA, both_sems],
    )

    intra_ins = [turn, (cumul, vm), (queries, hbm), (out_grad, hbm), (k, vm), (v, vm)]
    intra_outs = [
        ((heads, tokens, tokens), BF16, vm),
        (flat, F32, vm),
        (flat, F32, vm),
        (flat, F32, vm),
        ((heads, 2 * LANES, tokens), BF16, vm),
        (flat, BF16, vm),
        (flat, BF16, vm),
    ]
    inside = call(on_turn(intra_kernel, 0), "intra_early", intra_ins, intra_outs, [both_sems])
    send, inside = lax.optimization_barrier((send, inside))
    before, through = call(
        scan_kernel, "scan", [(exchange(send), vm)], [(pieces, F32, vm), ((ring, LANES), F32, vm)]
    )
    state_in = exchange(before).reshape(heads, LANES, LANES)
    state_in, inside = lax.optimization_barrier((state_in, inside))
    inside = call(on_turn(intra_kernel, 1), "intra_late", intra_ins, intra_outs, [both_sems], inside)
    probs, intra, grow, tail, pull, q, og = inside
    attn, sums = call(
        attn_kernel,
        "attn",
        [(q, vm), (state_in, vm), (intra, vm), (grow, vm), (gain_row, vm), (og, vm)],
        [(flat, F32, vm), ((others, 8, LANES), F32, vm)],
        [pltpu.VMEM((tokens, LANES), F32), pltpu.VMEM((tokens, LANES), F32)],
    )
    sums = lax.all_to_all(sums, "dp", 0, 0, tiled=True)
    grad, send, inv_rms = call(
        functools.partial(grad_kernel, features),
        "grad",
        [(pull, vm), (attn, vm), (gain_row, vm), (og, vm), (sums, vm)],
        [(flat, BF16, vm), (packed, F32, vm), ((tokens, LANES), F32, vm)],
        [pltpu.VMEM((tokens, LANES), F32)],
    )
    back_ins = [
        turn, (cumul, vm), (q, vm), (k, vm), (v, vm), (grad, vm), (probs, vm), (state_in, vm),
        (grow, vm), (attn, vm), (gain_row, vm), (inv_rms, vm),
    ]
    back_outs = [(flat, BF16, hbm), (flat, BF16, hbm), (flat, F32, vm), (flat, F32, vm)]
    back_scratch = [pltpu.VMEM(flat, BF16), pltpu.VMEM(flat, BF16), both_sems]
    inside = call(on_turn(intra_back_kernel, 0), "back_early", back_ins, back_outs, back_scratch)
    send, inside = lax.optimization_barrier((send, inside))
    after = call(
        scan_back_kernel, "scan_back", [(exchange(send), vm), (through, vm)], [(packed, F32, vm)]
    )[0]
    flow = exchange(after)
    flow, inside = lax.optimization_barrier((flow, inside))
    inside = call(on_turn(intra_back_kernel, 1), "back_late", back_ins, back_outs, back_scratch, inside)
    dq, normed, dk, dv = inside
    dk, dv, gain_grad = call(
        finish_kernel,
        "finish",
        [(k, vm), (v, vm), (dk, vm), (dv, vm), (tail, vm), (flow, vm)],
        [(flat, BF16, hbm), (flat, BF16, hbm), ((heads, LANES), F32, vm)],
        [pltpu.VMEM(flat, BF16), pltpu.VMEM(flat, BF16), both_sems],
    )
    return normed, dq, dk, dv, gain_grad.reshape(wide)


def solution(mesh):
    placed = (
        P("seq", "dp"),
        P("seq", "dp"),
        P("seq", "dp"),
        P("seq", "dp"),
        P("dp"),
        P("seq", "dp"),
    )
    return jax.shard_map(
        on_device,
        mesh=mesh,
        in_specs=placed,
        out_specs=(P("seq", "dp"), P("seq", "dp"), P("seq", "dp"), P("seq", "dp"), P("dp")),
        check_vma=False,
    )
```

time: 441 us -> 112 us (0.25); the launches traced: 435 us -> 112 us
  waiting for transfers between devices: 135 us -> 0 us
  other arithmetic: 86.9 us -> 0 us
  blocking collectives: 140 us -> 89.4 us
  matrix products: 37.6 us -> 0 us
  Pallas kernels: 0 us -> 21.1 us
  local copies, waits for them, and re-layouts: 18.7 us -> 0.61 us
  between operations: 14.2 us -> 0.87 us
    all_gather x2 -> x0, waiting for transfers between devices: 135 us -> none  [carried_in(): everything = jax.tree.map(lambda part: lax.all_gather(part, axis), x)]
    psum x3 -> x0, blocking collectives: 100 us -> none  [the longest x1 73.4 us: on_device(): gain_grad = lax.psum(gain_part, 'seq')]
    all_to_all x0 -> x5, blocking collectives: none -> 89.4 us  [the longest x4 79.8 us: exchange(): lax.all_to_all(x.reshape(-1), 'seq', 0, 0, tiled=True).reshape(x.shape)]
    select_n x64 -> x0, other arithmetic: 75.3 us -> none  [hop(): return jax.tree.map(lambda a, b: jnp.where(reached, a, b), new, before)]
    all_gather x1 -> x0, blocking collectives: 40.3 us -> none  [carried_in(): everything = jax.tree.map(lambda part: lax.all_gather(part, axis), x)]
    dot_general x12 -> x0, matrix products: 37.6 us -> none  [the longest x1 4.89 us: intra_backward(): jnp.einsum('hts,thd->shd', probs, g_blk, preferred_element_type=jnp.float32)]
    pallas_call x0 -> x10, Pallas kernels: none -> 21.1 us  [call(): pl.pallas_call(body, in_specs=[place(space) for space in spaces], out_spe...]
    unnamed x22 -> x2, local copies, waits for them, and re-layouts: 9.85 us -> 0.61 us
  transfers between devices with their start and end apart: 2 -> 0, of which waited for: 2 -> 0; matrix products, arithmetic and copies ran while one was open for 6% -> 0% of each run, Pallas kernels for 0% -> 0%
where the time goes in v2:
time: 112 us
  blocking collectives  89.4 us (80%)
  Pallas kernels  21.1 us (19%)
    all_to_all x4, blocking collectives, exchange(): lax.all_to_all(x.reshape(-1), 'seq', 0, 0, tiled=True).reshape(x.shape)  79.8 us
    pallas_call x10, Pallas kernels, call(): pl.pallas_call(body, in_specs=[place(space) for space in spaces], out_spe...  21.1 us
    all_to_all x1, blocking collectives, on_device(): sums = lax.all_to_all(sums, 'dp', 0, 0, tiled=True)  9.57 us

profile of v2, /device:TPU:32, one launch (start us, length us, event | category | flops | bytes accessed | tf_op | source)
XLA Modules:
  0.0 111.9 jit_solution(7254414865531580365)
XLA Ops:
  0.6 3.4 %front.1 = (f32[8,512]{1,0:T(8,128)S(1)}, f32[1056,128]{1,0:T(8,128)S(1)}, bf16[512,1024]{1,0:T(8,128)(2,1)S(1)}, bf16[512,1024]{1,0:T(8,128)(2,1)S(1)}) custom-call(f32[8,512]{1,0:T(8,128)} %bitcast.26, bf16[512,1024]{1,0:T(8,128)(2,1)} %k_hbm.1, bf16[512,1024]{1,0:T(8,128)(2,1)} %v_hbm.1), custom_call_target="tpu_custom_call" | custom-call | tf_op jit(solution)/shard_map/front/pallas_call | solution.py:281
  4.0 4.6 %intra_early.1 = (bf16[8,512,512]{2,1,0:T(8,128)(2,1)S(1)}, f32[512,1024]{1,0:T(8,128)S(1)}, f32[512,1024]{1,0:T(8,128)S(1)}, f32[512,1024]{1,0:T(8,128)S(1)}, b...) custom-call(s32[1]{0:T(128)} %bitcast.core_ref.refs_0_, ...), custom_call_target="tpu_custom_call" | custom-call | tf_op jit(solution)/shard_map/intra_early/pallas_call | solution.py:281
  8.6 25.3 %all_to_all.41 = f32[32,4224,1]{1,2,0:T(1,128)S(1)} all-to-all(f32[32,4224,1]{1,2,0:T(1,128)S(1)} %bitcast.19), channel_id=1, replica_groups=mesh['seq'=32,'dp'=8] {'seq'}, dimensions={0} | all-to-all | bytes 1081344 | tf_op jit(solution)/shard_map/all_to_all | solution.py:294
  33.9 0.1 scan.1
  34.0 17.9 %all_to_all.42 = f32[32,4096,1]{1,2,0:T(1,128)S(1)} all-to-all(f32[32,4096,1]{1,2,0:T(1,128)S(1)} %bitcast.21), channel_id=1, replica_groups=mesh['seq'=32,'dp'=8] {'seq'}, dimensions={0} | all-to-all | bytes 1048576 | tf_op jit(solution)/shard_map/all_to_all | solution.py:294
  51.9 0.0 copy-start
  51.9 0.1 intra_late.1
  52.0 0.6 copy-done
  52.6 1.5 %attn.1 = (f32[512,1024]{1,0:T(8,128)S(1)}, f32[8,8,128]{2,1,0:T(8,128)S(1)}) custom-call(bf16[512,1024]{1,0:T(8,128)(2,1)S(1)} %get-tuple-element.94.q_ref.refs_1_.refs_2_, f32[8,128,128]{2,1,0:T(8,128)S(1)} %bitcast.12, f32[512,1024]{1,0:T(8,128)S(1)} %get-tuple-element.97.intra_ref, f32[512,1024]{1,0:T(8,128)S(1)} %get-tuple-element.98.grow_ref.refs_7_.refs_8_, ...), custom_call_target="tpu_custom_call" | custom-call | tf_op jit(solution)/shard_map/attn/pallas_call | solution.py:281
  54.1 9.6 %all_to_all.43.sums_ref = f32[8,8,128]{2,1,0:T(8,128)S(1)} all-to-all(f32[8,8,128]{2,1,0:T(8,128)S(1)} %get-tuple-element.101), channel_id=1, replica_groups=mesh['seq'=32,'dp'=8] {'dp'}, dimensions={0} | all-to-all | bytes 65536 | tf_op jit(solution)/shard_map/all_to_all | solution.py:347
  63.7 1.5 %grad.1 = (bf16[512,1024]{1,0:T(8,128)(2,1)S(1)}, f32[1056,128]{1,0:T(8,128)S(1)}, f32[512,128]{1,0:T(8,128)S(1)}) custom-call(bf16[8,256,512]{2,1,0:T(8,128)(2,1)S(1)} %get-tuple-element.95.pull_ref, f32[512,1024]{1,0:T(8,128)S(1)} %get-tuple-element.100.attn_ref.refs_8_.refs_9_, f32[1,1024]{1,0:T(1,128)S(1)} %bitcast.23, ...), custom_call_target="tpu_custom_call" | custom-call | tf_op jit(solution)/shard_map/grad/pallas_call | solution.py:281
  65.1 7.0 %back_early.1 = (bf16[512,1024]{1,0:T(8,128)(2,1)}, bf16[512,1024]{1,0:T(8,128)(2,1)}, f32[512,1024]{1,0:T(8,128)S(1)}, f32[512,1024]{1,0:T(8,128)S(1)}) custom-call(s32[1]{0:T(128)} %bitcast.core_ref.refs_0_, f32[8,512]{1,0:T(8,128)S(1)} %get-tuple-element.67.refs_0_.refs_1_, bf16[512,1024]{1,0:T(8,128)(2,1)S(1)} %get-tuple-element.94.q_ref.refs_1_.refs_2_, ...), custom_call_target="tpu_custom_call" | custom-call | tf_op jit(solution)/shard_map/back_early/pallas_call | solution.py:281
  72.2 18.4 %all_to_all.44 = f32[32,4224,1]{1,2,0:T(1,128)S(1)} all-to-all(f32[32,4224,1]{1,2,0:T(1,128)S(1)} %bitcast.20), channel_id=1, replica_groups=mesh['seq'=32,'dp'=8] {'seq'}, dimensions={0} | all-to-all | bytes 1081344 | tf_op jit(solution)/shard_map/all_to_all | solution.py:294
  90.6 0.1 scan_back.1
  90.7 18.1 %all_to_all.45 = f32[32,4224,1]{1,2,0:T(1,128)S(1)} all-to-all(f32[32,4224,1]{1,2,0:T(1,128)S(1)} %bitcast.18), channel_id=1, replica_groups=mesh['seq'=32,'dp'=8] {'seq'}, dimensions={0} | all-to-all | bytes 1081344 | tf_op jit(solution)/shard_map/all_to_all | solution.py:294
  108.8 0.1 back_late.1
  108.9 2.8 %finish.1 = (bf16[512,1024]{1,0:T(8,128)(2,1)}, bf16[512,1024]{1,0:T(8,128)(2,1)}, f32[8,128]{1,0:T(8,128)}) custom-call(bf16[512,1024]{1,0:T(8,128)(2,1)S(1)} %get-tuple-element.68.refs_3_.refs_4_.refs_2_.k_ref, bf16[512,1024]{1,0:T(8,128)(2,1)S(1)} %get-tuple-element.69.refs_4_.refs_5_.refs_3_.v_ref, f32[512,1024]{1,0:T(8,128)S(1)} %get-tuple-element.122.dk_in_ref, ...), custom_call_target="tpu_custom_call" | custom-call | tf_op jit(solution)/shard_map/finish/pallas_call | solution.py:281
Async XLA Ops:
  51.9 0.7 copy-start

commit v3 on v2

v3 whole, which is shorter than its diff:
```python
import functools

import jax
import jax.numpy as jnp
from jax import lax
from jax.experimental import pallas as pl
from jax.experimental.pallas import tpu as pltpu
from jax.sharding import PartitionSpec as P

BLOCK = 512
EPSILON = 1e-06
HIGH = lax.Precision.HIGHEST
LANES = 128
GROUP = 2
TALL = 2 * LANES
QUARTER = LANES // 4
PIECE = QUARTER + 1
F32 = jnp.float32
BF16 = jnp.bfloat16
VMEM_LIMIT = 16 * 1024 * 1024


def contract(a, b, dim_a, dim_b, precision=None):
    return lax.dot_general(
        a, b, (((dim_a,), (dim_b,)), ((), ())), precision=precision, preferred_element_type=F32
    )


def halves(x, axis):
    high = x.astype(BF16)
    low = (x - high.astype(F32)).astype(BF16)
    return jnp.concatenate([high, low], axis=axis)


def down(row):
    parts = []
    for at in range(0, row.shape[1], LANES):
        piece = jnp.broadcast_to(row[:, at : at + LANES], (LANES, LANES))
        parts.append(piece.T)
    return jnp.concatenate(parts, axis=0)


def cols(head, count=1):
    return slice(head * LANES, (head + count) * LANES)


def pack(send_ref, head, update, extra):
    for quarter in range(4):
        first = (head * 4 + quarter) * PIECE
        send_ref[first : first + QUARTER, :] = update[quarter * QUARTER : (quarter + 1) * QUARTER]
        send_ref[first + QUARTER : first + PIECE, :] = extra


def row_copies(src, dst, sems):
    return [
        pltpu.make_async_copy(src.at[cols(part)], dst.at[cols(part)], sems.at[part])
        for part in range(src.shape[0] // LANES)
    ]


def intra(cumul_ref, k_ref, v_ref, q_ref, table_ref, probs_ref, intra_ref, grow_ref, tail_ref, pull_ref):
    heads, tokens = cumul_ref.shape
    place_t = lax.broadcasted_iota(jnp.int32, (LANES, LANES), 0)
    place_s = lax.broadcasted_iota(jnp.int32, (LANES, LANES), 1)
    lower = place_t >= place_s
    empty = jnp.zeros((LANES, LANES), F32)
    for head in range(heads):
        row = cumul_ref[head : head + 1, :]
        last = row[:, tokens - 1 :]
        column = down(row)
        mine = cols(head)
        grow_ref[:, mine] = jnp.exp(column)
        tail_ref[:, mine] = jnp.exp(last - column)
        pull_ref[head] = halves(q_ref[:, mine].T.astype(F32) * jnp.exp(row), 0)
        for at in range(0, tokens, TALL):
            end = at + TALL
            bands = []
            for t in range(at // LANES, end // LANES):
                tiles = []
                for s in range(end // LANES):
                    spread = column[cols(t)] - row[:, cols(s)]
                    if s < t:
                        tiles.append(jnp.exp(spread))
                    else:
                        tiles.append(jnp.where(lower, jnp.exp(spread), F32(0.0)) if s == t else empty)
                bands.append(jnp.concatenate(tiles, axis=1))
            weights = jnp.concatenate(bands, axis=0)
            table_ref[head, at:end, :end] = weights
            scores = contract(q_ref[at:end, mine], k_ref[:end, mine], 1, 1)
            probs = (weights * scores).astype(BF16)
            probs_ref[head, :end, at:end] = probs.T
            intra_ref[at:end, mine] = contract(probs, v_ref[:end, mine], 1, 0)


def front_kernel(
    core_ref, a_hbm, k_hbm, v_hbm, q_hbm, og_hbm,
    cumul_ref, send_ref, k_ref, v_ref, table_ref, probs_ref, intra_ref, grow_ref, tail_ref, pull_ref, q_ref, og_ref,
    a_ref, update_ref, a_sem, sems,
):
    heads, tokens = a_ref.shape
    a_copy = pltpu.make_async_copy(a_hbm, a_ref, a_sem)
    a_copy.start()
    k_copies = row_copies(k_hbm, k_ref, sems.at[0])
    v_copies = row_copies(v_hbm, v_ref, sems.at[1])
    late = row_copies(q_hbm, q_ref, sems.at[2]) + row_copies(og_hbm, og_ref, sems.at[3])
    for part in range(tokens // LANES):
        k_copies[part].start()
        v_copies[part].start()

    @pl.when(core_ref[0] == 0)
    def _():
        for copy in late:
            copy.start()

    place_s = lax.broadcasted_iota(jnp.int32, (LANES, LANES), 0)
    place_t = lax.broadcasted_iota(jnp.int32, (LANES, LANES), 1)
    upper = (place_s <= place_t).astype(F32)
    before = jnp.zeros((heads, 1), F32)
    a_copy.wait()
    for at in range(0, tokens, LANES):
        piece = contract(a_ref[:, at : at + LANES], upper, 1, 0, HIGH) + before
        before = piece[:, LANES - 1 :]
        cumul_ref[:, at : at + LANES] = piece
    for at in range(0, tokens, TALL):
        end = at + TALL
        for copies in (k_copies, v_copies):
            for copy in copies[at // LANES : end // LANES]:
                copy.wait()
        for head in range(heads):
            mine = cols(head)
            row = cumul_ref[head : head + 1, :]
            last = row[:, tokens - 1 :]
            k_tail = k_ref[at:end, mine].T.astype(F32) * jnp.exp(last - row[:, at:end])
            both = contract(halves(k_tail, 0), v_ref[at:end, mine], 1, 0)
            update = both[:LANES] + both[LANES:]
            if at:
                update = update + update_ref[head]
            if end < tokens:
                update_ref[head] = update
            else:
                pack(send_ref, head, update, jnp.broadcast_to(last, (1, LANES)))

    @pl.when(core_ref[0] == 0)
    def _():
        for copy in late[:4]:
            copy.wait()
        intra(cumul_ref, k_ref, v_ref, q_ref, table_ref, probs_ref, intra_ref, grow_ref, tail_ref, pull_ref)
        for copy in late[4:]:
            copy.wait()


def attn_kernel(
    core_ref, q_hbm, og_hbm, cumul_ref, k_ref, v_ref, state_ref, gain_ref,
    table_ref, probs_ref, intra_ref, grow_ref, tail_ref, pull_ref, q_ref, og_ref, attn_ref, sums_ref,
    sq_ref, gd_ref, sems,
):
    @pl.when(core_ref[0] == 1)
    def _():
        late = row_copies(q_hbm, q_ref, sems.at[0]) + row_copies(og_hbm, og_ref, sems.at[1])
        for copy in late:
            copy.start()
        for copy in late[:4]:
            copy.wait()
        intra(cumul_ref, k_ref, v_ref, q_ref, table_ref, probs_ref, intra_ref, grow_ref, tail_ref, pull_ref)
        for copy in late[4:]:
            copy.wait()

    for at in range(0, state_ref.shape[0], GROUP):
        squares = jnp.zeros(sq_ref.shape, F32) if at == 0 else sq_ref[...]
        gdot = jnp.zeros(gd_ref.shape, F32) if at == 0 else gd_ref[...]
        for head in range(at, at + GROUP):
            mine = cols(head)
            q_one = q_ref[:, mine]
            carried = contract(jnp.concatenate([q_one, q_one], axis=1), halves(state_ref[head], 0), 1, 0)
            attn = intra_ref[:, mine] + grow_ref[:, mine] * carried
            attn_ref[:, mine] = attn
            squares = squares + attn * attn
            gdot = gdot + gain_ref[:, mine] * og_ref[:, mine].astype(F32) * attn
        sq_ref[...] = squares
        gd_ref[...] = gdot
    ones = jnp.ones((8, LANES), F32)
    sq_row = contract(ones, sq_ref[...], 1, 1, HIGH)
    gd_row = contract(ones, gd_ref[...], 1, 1, HIGH)
    pieces = [sq_row[:1, at : at + LANES] for at in range(0, BLOCK, LANES)]
    pieces += [gd_row[:1, at : at + LANES] for at in range(0, BLOCK, LANES)]
    whole = jnp.concatenate(pieces, axis=0)
    sums_ref[...] = jnp.broadcast_to(whole[None], sums_ref.shape)


def intra_back(
    q_ref, k_ref, v_ref, grad_ref, table_ref, probs_ref, state_ref, grow_ref, attn_ref, gain_ref, inv_ref,
    dq_hbm, normed_hbm, dk_ref, dv_ref, dq_ref, normed_ref, errs_ref, sems,
):
    heads, tokens = table_ref.shape[:2]
    copies = row_copies(normed_ref, normed_hbm, sems.at[0])
    for part in range(tokens // LANES):
        rows = cols(part)
        inv_rms = jnp.concatenate([inv_ref[rows, :]] * heads, axis=1)
        normed_ref[rows, :] = (attn_ref[rows, :] * inv_rms * gain_ref[...]).astype(BF16)
        copies[part].start()
    dq_copies = row_copies(dq_ref, dq_hbm, sems.at[1])
    for at in range(0, tokens, TALL):
        end = at + TALL
        for head in range(heads):
            mine = cols(head)
            grad = grad_ref[at:end, mine]
            scores = contract(grad, v_ref[:end, mine], 1, 1)
            errs = (table_ref[head, at:end, :end] * scores).astype(BF16)
            errs_ref[head, at:end, :end] = errs
            carried = contract(jnp.concatenate([grad, grad], axis=1), halves(state_ref[head], 1), 1, 1)
            dq = contract(errs, k_ref[:end, mine], 1, 0) + grow_ref[at:end, mine] * carried
            dq_ref[at:end, mine] = dq.astype(BF16)
        for part in range(at // LANES, end // LANES):
            dq_copies[part].start()
    for head in range(heads):
        mine = cols(head)
        for at in range(0, tokens, TALL):
            end = at + TALL
            dk_ref[at:end, mine] = contract(errs_ref[head, at:, at:end], q_ref[at:, mine], 0, 0)
            dv_ref[at:end, mine] = contract(probs_ref[head, at:end, at:], grad_ref[at:, mine], 1, 0)
    return copies + dq_copies


def grad_kernel(
    features, core_ref, q_ref, k_ref, v_ref, table_ref, probs_ref, state_ref, grow_ref, attn_ref, gain_ref,
    pull_ref, og_ref, sums_ref,
    grad_ref, send_ref, inv_ref, dq_hbm, normed_hbm, dk_ref, dv_ref, back_ref, dq_ref, normed_ref, errs_ref, sems,
):
    whole = jnp.sum(sums_ref[...], axis=0)
    inv_rms = lax.rsqrt(whole[:4] / features + EPSILON)
    back = inv_rms * inv_rms * inv_rms * whole[4:] / features
    for at in range(4):
        inv_ref[cols(at), :] = jnp.broadcast_to(inv_rms[at : at + 1], (LANES, LANES)).T
        back_ref[cols(at), :] = jnp.broadcast_to(back[at : at + 1], (LANES, LANES)).T
    for head in range(pull_ref.shape[0]):
        mine = cols(head)
        og = og_ref[:, mine].astype(F32)
        grad = inv_ref[...] * gain_ref[:, mine] * og - attn_ref[:, mine] * back_ref[...]
        grad = grad.astype(BF16)
        grad_ref[:, mine] = grad
        both = contract(pull_ref[head], grad, 1, 0)
        update = both[:LANES] + both[LANES:]
        gain_part = jnp.sum(og * (attn_ref[:, mine] * inv_ref[...]), axis=0, keepdims=True)
        pack(send_ref, head, update, gain_part)

    @pl.when(core_ref[0] == 0)
    def _():
        copies = intra_back(
            q_ref, k_ref, v_ref, grad_ref, table_ref, probs_ref, state_ref, grow_ref, attn_ref, gain_ref, inv_ref,
            dq_hbm, normed_hbm, dk_ref, dv_ref, dq_ref, normed_ref, errs_ref, sems,
        )
        for copy in copies:
            copy.wait()


def finish_kernel(
    core_ref, q_ref, k_ref, v_ref, table_ref, probs_ref, state_ref, grow_ref, attn_ref, gain_ref, grad_ref, inv_ref,
    tail_ref, flow_ref,
    dq_hbm, normed_hbm, dk32_ref, dv32_ref, dk_hbm, dv_hbm, gain_grad_ref,
    dq_ref, normed_ref, dk_ref, dv_ref, errs_ref, wide_ref, high_ref, sems,
):
    @pl.when(core_ref[0] == 1)
    def _():
        intra_back(
            q_ref, k_ref, v_ref, grad_ref, table_ref, probs_ref, state_ref, grow_ref, attn_ref, gain_ref, inv_ref,
            dq_hbm, normed_hbm, dk32_ref, dv32_ref, dq_ref, normed_ref, errs_ref, sems,
        )

    heads, tokens = table_ref.shape[:2]
    for head in range(heads):
        firsts = [(head * 4 + quarter) * PIECE for quarter in range(4)]
        flow = jnp.concatenate([flow_ref[first : first + QUARTER, :] for first in firsts], axis=0)
        wide_ref[head] = halves(flow, 1)
        high_ref[head] = halves(flow, 0)
        gain_grad_ref[head : head + 1, :] = flow_ref[firsts[0] + QUARTER : firsts[0] + PIECE, :]
    dk_copies = row_copies(dk_ref, dk_hbm, sems.at[2])
    dv_copies = row_copies(dv_ref, dv_hbm, sems.at[3])
    for part in range(tokens // LANES):
        rows = cols(part)
        for head in range(heads):
            mine = cols(head)
            k_one, v_one = k_ref[rows, mine], v_ref[rows, mine]
            dk = contract(jnp.concatenate([v_one, v_one], axis=1), wide_ref[head], 1, 1)
            dv = contract(jnp.concatenate([k_one, k_one], axis=1), high_ref[head], 1, 0)
            tail = tail_ref[rows, mine]
            dk_ref[rows, mine] = (dk32_ref[rows, mine] + tail * dk).astype(BF16)
            dv_ref[rows, mine] = (dv32_ref[rows, mine] + tail * dv).astype(BF16)
        dk_copies[part].start()
        dv_copies[part].start()

    @pl.when(core_ref[0] == 1)
    def _():
        for copy in row_copies(normed_ref, normed_hbm, sems.at[0]) + row_copies(dq_ref, dq_hbm, sems.at[1]):
            copy.wait()

    for copy in dk_copies + dv_copies:
        copy.wait()


def scan_kernel(got_ref, out_ref, through_ref):
    count = out_ref.shape[0]
    state = jnp.zeros((QUARTER, LANES), F32)
    for at in range(count):
        out_ref[at] = state
        first = at * PIECE
        through = jnp.exp(got_ref[first + QUARTER : first + PIECE, :])
        through_ref[at : at + 1, :] = through
        state = through * state + got_ref[first : first + QUARTER, :]


def scan_back_kernel(got_ref, through_ref, out_ref):
    count = through_ref.shape[0]
    state = jnp.zeros((QUARTER, LANES), F32)
    gain = jnp.zeros((1, LANES), F32)
    for at in reversed(range(count)):
        first = at * PIECE
        out_ref[first : first + QUARTER, :] = state
        state = through_ref[at : at + 1, :] * state + got_ref[first : first + QUARTER, :]
        gain = gain + got_ref[first + QUARTER : first + PIECE, :]
    for at in range(count):
        out_ref[at * PIECE + QUARTER : (at + 1) * PIECE, :] = gain


def call(kernel, name, ins, outs, scratch=(), into=None):
    place = lambda space: pl.BlockSpec(memory_space=space)
    pin = lambda array, space: pltpu.with_memory_space_constraint(array, space) if space == pltpu.HBM else array
    spaces = [space for _, space in ins]
    arrays = [pin(array, space) for array, space in ins]
    aliases = {}
    body = kernel
    if into is not None:
        known, count = len(ins), len(into)
        aliases = {known + at: at for at in range(count)}
        spaces += [space for _, _, space in outs[:count]]
        arrays += [pin(array, space) for array, (_, _, space) in zip(into, outs)]
        body = lambda *refs: kernel(*refs[:known], *refs[known + count :])
    return pl.pallas_call(
        body,
        in_specs=[place(space) for space in spaces],
        out_specs=[place(space) for _, _, space in outs],
        out_shape=[jax.ShapeDtypeStruct(shape, dtype) for shape, dtype, _ in outs],
        scratch_shapes=list(scratch),
        input_output_aliases=aliases,
        compiler_params=pltpu.CompilerParams(vmem_limit_bytes=VMEM_LIMIT),
        name=name,
    )(*arrays)


def exchange(x):
    return lax.all_to_all(x.reshape(-1), "seq", 0, 0, tiled=True).reshape(x.shape)


def on_device(queries, key_vecs, value_vecs, log_decay, norm_gain, out_grad):
    tokens, wide = queries.shape
    heads = log_decay.shape[1]
    ring = lax.axis_size("seq")
    others = lax.axis_size("dp")
    features = wide * others
    parts = tokens // LANES
    gain_row = norm_gain.reshape(1, wide)
    vm, hbm = pltpu.VMEM, pltpu.HBM
    core = ((lax.axis_index("dp") & 1).astype(jnp.int32).reshape(1), pltpu.SMEM)
    flat = (tokens, wide)
    square = (heads, tokens, tokens)
    packed = (ring * PIECE, LANES)

    inside_outs = [
        (square, F32, vm),
        (square, BF16, vm),
        (flat, F32, vm),
        (flat, F32, vm),
        (flat, F32, vm),
        ((heads, 2 * LANES, tokens), BF16, vm),
        (flat, BF16, vm),
        (flat, BF16, vm),
    ]
    cumul, send, k, v, *inside = call(
        front_kernel,
        "front",
        [core, (log_decay.T, hbm), (key_vecs, hbm), (value_vecs, hbm), (queries, hbm), (out_grad, hbm)],
        [((heads, tokens), F32, vm), (packed, F32, vm), (flat, BF16, vm), (flat, BF16, vm)] + inside_outs,
        [
            pltpu.VMEM((heads, tokens), F32),
            pltpu.VMEM((heads, LANES, LANES), F32),
            pltpu.SemaphoreType.DMA,
            pltpu.SemaphoreType.DMA((4, parts)),
        ],
    )
    before, through = call(
        scan_kernel,
        "scan",
        [(exchange(send), vm)],
        [((ring, QUARTER, LANES), F32, vm), ((ring, LANES), F32, vm)],
    )
    state_in = exchange(before).reshape(heads, LANES, LANES)
    *inside, attn, sums = call(
        attn_kernel,
        "attn",
        [core, (queries, hbm), (out_grad, hbm), (cumul, vm), (k, vm), (v, vm), (state_in, vm), (gain_row, vm)],
        inside_outs + [(flat, F32, vm), ((others, 8, LANES), F32, vm)],
        [pltpu.VMEM((tokens, LANES), F32)] * 2 + [pltpu.SemaphoreType.DMA((2, parts))],
        inside,
    )
    table, probs, intra_attn, grow, tail, pull, q, og = inside
    sums = lax.all_to_all(sums, "dp", 0, 0, tiled=True)
    block_ins = [
        core, (q, vm), (k, vm), (v, vm), (table, vm), (probs, vm), (state_in, vm), (grow, vm), (attn, vm), (gain_row, vm)
    ]
    block_outs = [(flat, BF16, hbm), (flat, BF16, hbm), (flat, F32, vm), (flat, F32, vm)]
    grad, send, inv_rms, *inside = call(
        functools.partial(grad_kernel, features),
        "grad",
        block_ins + [(pull, vm), (og, vm), (sums, vm)],
        [(flat, BF16, vm), (packed, F32, vm), ((tokens, LANES), F32, vm)] + block_outs,
        [
            pltpu.VMEM((tokens, LANES), F32),
            pltpu.VMEM(flat, BF16),
            pltpu.VMEM(flat, BF16),
            pltpu.VMEM(square, BF16),
            pltpu.SemaphoreType.DMA((2, parts)),
        ],
    )
    after = call(
        scan_back_kernel, "scan_back", [(exchange(send), vm), (through, vm)], [(packed, F32, vm)]
    )[0]
    dq, normed, _, _, dk, dv, gain_grad = call(
        finish_kernel,
        "finish",
        block_ins + [(grad, vm), (inv_rms, vm), (tail, vm), (exchange(after), vm)],
        block_outs + [(flat, BF16, hbm), (flat, BF16, hbm), ((heads, LANES), F32, vm)],
        [pltpu.VMEM(flat, BF16)] * 4
        + [
            pltpu.VMEM(square, BF16),
            pltpu.VMEM((heads, LANES, 2 * LANES), BF16),
            pltpu.VMEM((heads, 2 * LANES, LANES), BF16),
            pltpu.SemaphoreType.DMA((4, parts)),
        ],
        inside,
    )
    return normed, dq, dk, dv, gain_grad.reshape(wide)


def solution(mesh):
    placed = (
        P("seq", "dp"),
        P("seq", "dp"),
        P("seq", "dp"),
        P("seq", "dp"),
        P("dp"),
        P("seq", "dp"),
    )
    return jax.shard_map(
        on_device,
        mesh=mesh,
        in_specs=placed,
        out_specs=(P("seq", "dp"), P("seq", "dp"), P("seq", "dp"), P("seq", "dp"), P("dp")),
        check_vma=False,
    )
```

time: 112 us -> 110 us (0.982)
  Pallas kernels: 21.1 us -> 18.8 us
    pallas_call x10 -> x6, Pallas kernels: 21.1 us -> 18.8 us  [call(): pl.pallas_call(body, in_specs=[place(space) for space in spaces], out_spe...]
where the time goes in v3:
time: 110 us; the launch traced here: 109 us
  blocking collectives  89.6 us (81%)
  Pallas kernels  18.8 us (17%)
    all_to_all x4, blocking collectives, exchange(): lax.all_to_all(x.reshape(-1), 'seq', 0, 0, tiled=True).reshape(x.shape)  80.1 us
    pallas_call x6, Pallas kernels, call(): pl.pallas_call(body, in_specs=[place(space) for space in spaces], out_spe...  18.8 us
    all_to_all x1, blocking collectives, on_device(): sums = lax.all_to_all(sums, 'dp', 0, 0, tiled=True)  9.55 us

profile of v3, /device:TPU:32, one launch (start us, length us, event | category | flops | bytes accessed | tf_op | source)
XLA Modules:
  0.0 109.3 jit_solution(7122263587824911210)
XLA Ops:
  0.6 7.0 %front.1 = (f32[8,512]{1,0:T(8,128)S(1)}, f32[1056,128]{1,0:T(8,128)S(1)}, bf16[512,1024]{1,0:T(8,128)(2,1)S(1)}, bf16[512,1024]{1,0:T(8,128)(2,1)S(1)}, f32[8,5...) custom-call(s32[1]{0:T(128)} %bitcast.core_ref.refs_0_, ...), custom_call_target="tpu_custom_call" | custom-call | tf_op jit(solution)/shard_map/front/pallas_call | solution.py:337
  7.7 0.0 copy-start
  7.7 25.6 %all_to_all.41 = f32[32,4224,1]{1,2,0:T(1,128)S(1)} all-to-all(f32[32,4224,1]{1,2,0:T(1,128)S(1)} %bitcast.19), channel_id=1, replica_groups=mesh['seq'=32,'dp'=8] {'seq'}, dimensions={0} | all-to-all | bytes 1081344 | tf_op jit(solution)/shard_map/all_to_all | solution.py:350
  33.3 0.1 scan.1
  33.4 18.1 %all_to_all.42 = f32[32,4096,1]{1,2,0:T(1,128)S(1)} all-to-all(f32[32,4096,1]{1,2,0:T(1,128)S(1)} %bitcast.21), channel_id=1, replica_groups=mesh['seq'=32,'dp'=8] {'seq'}, dimensions={0} | all-to-all | bytes 1048576 | tf_op jit(solution)/shard_map/all_to_all | solution.py:350
  51.5 0.0 copy-done
  51.5 1.6 %attn.1 = (f32[8,512,512]{2,1,0:T(8,128)S(1)}, bf16[8,512,512]{2,1,0:T(8,128)(2,1)S(1)}, f32[512,1024]{1,0:T(8,128)S(1)}, f32[512,1024]{1,0:T(8,128)S(1)}, f32[5...) custom-call(s32[1]{0:T(128)} %bitcast.core_ref.refs_0_, ...), custom_call_target="tpu_custom_call", output_to_operand_aliasing={{0}: (8, {}), {1}: (9, {}), {2}: (10, {}), {3}: (11, {}), {... | custom-call | tf_op jit(solution)/shard_map/attn/pallas_call | solution.py:337
  53.1 9.5 %all_to_all.43.sums_ref = f32[8,8,128]{2,1,0:T(8,128)S(1)} all-to-all(f32[8,8,128]{2,1,0:T(8,128)S(1)} %get-tuple-element.60), channel_id=1, replica_groups=mesh['seq'=32,'dp'=8] {'dp'}, dimensions={0} | all-to-all | bytes 65536 | tf_op jit(solution)/shard_map/all_to_all | solution.py:405
  62.7 7.0 %grad.1 = (bf16[512,1024]{1,0:T(8,128)(2,1)S(1)}, f32[1056,128]{1,0:T(8,128)S(1)}, f32[512,128]{1,0:T(8,128)S(1)}, bf16[512,1024]{1,0:T(8,128)(2,1)}, bf16[512,1...) custom-call(s32[1]{0:T(128)} %bitcast.core_ref.refs_0_, ...), custom_call_target="tpu_custom_call" | custom-call | tf_op jit(solution)/shard_map/grad/pallas_call | solution.py:337
  69.7 18.3 %all_to_all.44 = f32[32,4224,1]{1,2,0:T(1,128)S(1)} all-to-all(f32[32,4224,1]{1,2,0:T(1,128)S(1)} %bitcast.20), channel_id=1, replica_groups=mesh['seq'=32,'dp'=8] {'seq'}, dimensions={0} | all-to-all | bytes 1081344 | tf_op jit(solution)/shard_map/all_to_all | solution.py:350
  88.0 0.1 scan_back.1
  88.1 18.1 %all_to_all.45 = f32[32,4224,1]{1,2,0:T(1,128)S(1)} all-to-all(f32[32,4224,1]{1,2,0:T(1,128)S(1)} %bitcast.17), channel_id=1, replica_groups=mesh['seq'=32,'dp'=8] {'seq'}, dimensions={0} | all-to-all | bytes 1081344 | tf_op jit(solution)/shard_map/all_to_all | solution.py:350
  106.2 3.0 %finish.1 = (bf16[512,1024]{1,0:T(8,128)(2,1)}, bf16[512,1024]{1,0:T(8,128)(2,1)}, f32[512,1024]{1,0:T(8,128)S(1)}, f32[512,1024]{1,0:T(8,128)S(1)}, bf16[512,10...) custom-call(s32[1]{0:T(128)} %bitcast.core_ref.refs_0_, ...), custom_call_target="tpu_custom_call", output_to_operand_aliasing={{0}: (14, {}), {1}: (15, {}), {2}: (16, {}), {3}: (17, {})} | custom-call | tf_op jit(solution)/shard_map/finish/pallas_call | solution.py:337
Async XLA Ops:
  7.7 43.8 %copy-start = (f32[1024]{0:T(1024)S(1)}, f32[1024]{0:T(1024)}, u32[]{:S(2)}) copy-start(f32[1024]{0:T(1024)} %param.10) | copy-start | bytes 12292
